TPU v7x, 128 devices: a whole 4x4x4 slice. The times are simulated.
128 devices in a mesh: gx: 8 (over z, core), gy: 16 (over y, x).
Axes of the slice: x: 4, y: 4, z: 4, core: 2. Of those that a mesh axis runs over, the one named last changes fastest.
Arguments:
- seg_source: float32 [9, 64, 2048], P(None, 'gx', 'gy'), may hold values from -0.3125 to 0.3125
- seg_inverse: float32 [9, 9, 64, 2048], P(None, None, 'gx', 'gy')
- seg_outflow: float32 [9, 9, 64, 2048], P(None, None, 'gx', 'gy')
- well_len: int32 [64], P('gx'), may hold values from 1 to 2048, as said below
- perf_seg: int32 [8, 16, 16, 256], P('gx', 'gy'), may hold values from 0 to 1023, as said below
- perf_count: int32 [8, 16, 16], P('gx', 'gy'), may hold values from 0 to 256, as said below
- perf_coupling: float32 [9, 9, 8, 16, 16, 256], P(None, None, 'gx', 'gy'), may hold values from -3 to 3
- recv_cell: int32 [8, 16, 16, 256], P('gx', 'gy'), may hold values from 0 to 8191
- cell_cot: bfloat16 [9, 64, 128, 128], P(None, 'gx', 'gy'), may hold values from -6 to 6
- start_iterate: float32 [9, 64, 128, 128], P(None, 'gx', 'gy'), may hold values from -6 to 6
- accumulation: bfloat16 [9, 64, 128, 128], P(None, 'gx', 'gy'), may hold values from 0.049804688 to 0.5
- mobility: bfloat16 [9, 64, 128, 128], P(None, 'gx', 'gy'), may hold values from 0.19921875 to 2
- perm_x: float32 [64, 128, 128], P('gx', 'gy'), may hold values from 0.3 to 1.5
- perm_y: float32 [64, 128, 128], P('gx', 'gy'), may hold values from 0.3 to 1.5
- perm_z: float32 [64, 128, 128], P('gx', 'gy'), may hold values from 0.3 to 1.5
Outputs:
- seg_adjoint: float32 [9, 64, 2048], P(None, 'gx', 'gy')
- cell_adjoint: float32 [9, 64, 128, 128], P(None, 'gx', 'gy')
Inputs may be any that keep to these rules, and one draw needn't show every extreme that they name: perf_count[i, j, b] is 0 where |b - j| > 8 and equals 256 where b = j. `well_len`: every index of gx has a well of 2048 active segments. `perf_seg`: every row names a segment slot q of brick (i, j) whose segment is active: j * 128 + q % 128 < well_len[i * 8 + q // 128].
All inputs are finite; a program needn't handle non-finite values.
Results may differ from a plain program's by a relative error of at most 0.00035.
Values sent between devices are 32-bit elements; how exact they have to be, the bound alone decides.
No kernel may reach another device: no remote copies, remote signals or barrier semaphores. Data moves between devices by JAX's collectives and lax.ppermute only.
A program may use at most 128 MiB of HBM per device.

v0:
```python
import jax
import jax.numpy as jnp
from jax import lax
from jax.experimental import pallas as pl
from jax.experimental.pallas import tpu as pltpu
from jax.sharding import PartitionSpec as P

F32 = jnp.float32
BF16 = jnp.bfloat16
I32 = jnp.int32
NC = 9
OMEGA = 0.8
KEEP = 1.0 - OMEGA
BRICKS = 16
EARLY = 6
LATE = 5
TILE = (8, 128)
FIELDS = 21
EARLY_ROWS = 16 + FIELDS * 8 * EARLY
LATE_ROWS = 16 + NC * 8 * LATE
RATIO_AT = 12 * EARLY * 24
WIDE_ROWS = RATIO_AT + NC * LATE * 16
COLS = 8 + 2 * LATE
SLOT = 24

VMEM = pl.BlockSpec(memory_space=pltpu.VMEM)
SMEM = pl.BlockSpec(memory_space=pltpu.SMEM)


def lanes_of(shape=TILE):
    return lax.broadcasted_iota(I32, shape, 1)


def rows_of(shape=TILE):
    return lax.broadcasted_iota(I32, shape, 0)


def call(kernel, outs, scratch, specs, name, flops=1_000_000, limit=16):
    return pl.pallas_call(
        kernel,
        out_shape=outs,
        in_specs=specs,
        out_specs=jax.tree.map(lambda _: VMEM, outs),
        scratch_shapes=scratch,
        compiler_params=pltpu.CompilerParams(vmem_limit_bytes=limit * 1024 * 1024),
        cost_estimate=pl.CostEstimate(
            flops=flops, bytes_accessed=1_000_000, transcendentals=0
        ),
        name=name,
    )


def out(*shape):
    return jax.ShapeDtypeStruct(shape, F32)


def scan_kernel(len_ref, src, inv, outf, mats, vecs, head, rolled):
    lane = lanes_of()
    well = rows_of()
    length = jnp.zeros(TILE, I32)
    for w in range(8):
        length = jnp.where(well == w, len_ref[w], length)
    active = (lax.axis_index("gy") * 128 + lane < length).astype(F32)

    def start(c, _):
        row = [inv[j, c] for j in range(NC)]
        total = row[0] * src[0]
        for j in range(1, NC):
            total = total + row[j] * src[j]
        vecs[c] = active * total
        for k in range(NC):
            total = row[0] * outf[k, 0]
            for j in range(1, NC):
                total = total + row[j] * outf[k, j]
            mats[c * NC + k] = -active * total
        return 0

    lax.fori_loop(0, NC, start, 0)

    def step(i, _):
        gap = lax.shift_left(jnp.int32(1), i)
        keep = lane < 128 - gap
        for k in range(NC):
            for m in range(NC):
                moved = pltpu.roll(mats[k * NC + m], 128 - gap, 1)
                rolled[k * 10 + m] = jnp.where(keep, moved, 1.0 if k == m else 0.0)
            rolled[k * 10 + 9] = jnp.where(keep, pltpu.roll(vecs[k], 128 - gap, 1), 0.0)

        def rows(group, _):
            rows3 = [[mats[(group * 3 + a) * NC + k] for k in range(NC)] for a in range(3)]
            for m in range(10):
                right = [rolled[k * 10 + m] for k in range(NC)]
                for a in range(3):
                    total = rows3[a][0] * right[0]
                    for k in range(1, NC):
                        total = total + rows3[a][k] * right[k]
                    if m < NC:
                        mats[(group * 3 + a) * NC + m] = total
                    else:
                        vecs[group * 3 + a] = vecs[group * 3 + a] + total
            return 0

        return lax.fori_loop(0, 3, rows, 0)

    lax.fori_loop(0, 7, step, 0)
    packed = jnp.zeros(TILE, F32)
    for e in range(81):
        moved = mats[e] if e == 0 else pltpu.roll(mats[e], e, 1)
        packed = jnp.where(lane == e, moved, packed)
    for c in range(NC):
        packed = jnp.where(lane == 81 + c, pltpu.roll(vecs[c], 81 + c, 1), packed)
    for j in range(BRICKS):
        head[j] = packed


def rows_kernel(count_ref, mats, vecs, heads, perf_seg, coupling, lam, sent):
    row = rows_of()
    lane = lanes_of()
    me = lax.axis_index("gy")

    def hop(t, incoming):
        head = heads[BRICKS - 1 - t]
        after = []
        for c in range(NC):
            total = jnp.broadcast_to(head[:, 81 + c : 82 + c], TILE)
            for k in range(NC):
                at = c * NC + k
                total = total + jnp.broadcast_to(head[:, at : at + 1], TILE) * incoming[k]
            after.append(total)
        return tuple(after)

    nothing = tuple(jnp.zeros(TILE, F32) for _ in range(NC))
    incoming = lax.fori_loop(0, BRICKS - 1 - me, hop, nothing)
    for c in range(NC):
        total = vecs[c]
        for k in range(NC):
            total = total + mats[c * NC + k] * incoming[k]
        lam[c] = total
    for block in range(2):
        count = jnp.zeros(TILE, I32)
        for b in range(8):
            count = jnp.where(row == b, count_ref[block * 8 + b], count)
        for half in range(2):
            at = (slice(block * 8, block * 8 + 8), slice(half * 128, half * 128 + 128))
            slot = perf_seg[at]
            slot_well = lax.shift_right_logical(slot, 7)
            slot_lane = lax.bitwise_and(slot, 127)
            is_well = [slot_well == w for w in range(8)]
            picked = []
            for k in range(NC):
                total = jnp.zeros(TILE, F32)
                for w in range(8):
                    line = jnp.broadcast_to(lam[k, w : w + 1, :], TILE)
                    got = jnp.take_along_axis(line, slot_lane, axis=1)
                    total = jnp.where(is_well[w], got, total)
                picked.append(total)
            live = lane + half * 128 < count
            for c in range(NC):
                total = coupling[(0, c) + at] * picked[0]
                for k in range(1, NC):
                    total = total + coupling[(k, c) + at] * picked[k]
                total = jnp.where(live, total, 0.0)
                sent[pl.ds(block * 8 * SLOT + c * 2 + half, 8, stride=SLOT), :] = total


def early_pack_kernel(start, px, py, pz, accum, mobil, ratio, send_a, send_b):
    even = lax.rem(lax.axis_index("gy"), 2) == 0
    for i in range(NC * 4):
        at = slice(i * 16, i * 16 + 16)
        ratio[at, :] = accum[at, :].astype(F32) / mobil[at, :].astype(F32)
    for buffer in (send_a, send_b):
        buffer[0:8, :] = jnp.zeros(TILE, F32)
        buffer[EARLY_ROWS - 8 : EARLY_ROWS, :] = jnp.zeros(TILE, F32)
    perms = (px, py, pz)
    for f in range(FIELDS):
        for x in range(8):
            if f < NC:
                low, high = start[f, x, 0:EARLY, :], start[f, x, 8 - EARLY : 8, :]
            elif f < 12:
                low, high = perms[f - 9][x, 0:EARLY, :], perms[f - 9][x, 8 - EARLY : 8, :]
            else:
                base = ((f - 12) * 8 + x) * 8
                low, high = ratio[base : base + EARLY, :], ratio[base + 8 - EARLY : base + 8, :]
            at = 8 + (f * 8 + x) * EARLY
            send_a[at : at + EARLY, :] = jnp.where(even, high, low)
            send_b[at : at + EARLY, :] = jnp.where(even, low, high)


def early_wide_kernel(start, px, py, pz, ratio, recv_a, recv_b, wide, send_a, send_b):
    row = rows_of()
    gy = lax.axis_index("gy")
    even = lax.rem(gy, 2) == 0
    south_in = (gy > 0).astype(F32)
    north_in = (gy < BRICKS - 1).astype(F32)
    perms = (px, py, pz)
    for f in range(FIELDS):
        for x in range(8):
            at = 8 + (f * 8 + x) * EARLY
            low = slice(at - (8 - EARLY), at + EARLY)
            high = slice(at, at + 8)
            south = jnp.where(even, recv_b[low, :], recv_a[low, :])
            north = jnp.where(even, recv_a[high, :], recv_b[high, :])
            if f < NC:
                home = start[f, x]
            elif f < 12:
                home = perms[f - 9][x]
                south = south * south_in
                north = north * north_in
            else:
                base = ((f - 12) * 8 + x) * 8
                home = ratio[base : base + 8, :]
            wide[x, f, 0:8, :] = south
            wide[x, f, 8:16, :] = home
            wide[x, f, 16:24, :] = north
    even_x = lax.rem(lax.axis_index("gx"), 2) == 0
    for buffer, east in ((send_a, even_x), (send_b, jnp.logical_not(even_x))):
        first = jnp.where(east, 8 - EARLY, 0)
        for f in range(12):
            for d in range(EARLY):
                at = (d * 12 + f) * 24
                buffer[at : at + 24, :] = wide[first + d, f]
        first = jnp.where(east, 8 - LATE, 0)
        for d in range(LATE):
            for c in range(NC):
                at = RATIO_AT + (d * NC + c) * 16
                buffer[at : at + 8, :] = wide[first + d, 12 + c, 8:16, :]
                buffer[at + 8 : at + 16, :] = jnp.where(
                    row < 4, wide[first + d, 12 + c, 16:24, :], wide[first + d, 12 + c, 0:8, :]
                )


def north_of(tiles, row):
    south, home, north = (pltpu.roll(tile, 7, 0) for tile in tiles)
    last = row == 7
    return (jnp.where(last, home, south), jnp.where(last, north, home), north)


def south_of(tiles, row):
    south, home, north = (pltpu.roll(tile, 1, 0) for tile in tiles)
    first = row == 0
    return (south, jnp.where(first, south, home), jnp.where(first, home, north))


def early_kernel(
    wide, recv_a, recv_b, trans, gain, begin, begin_edge, iters, perms, ratios
):
    row = rows_of()
    lane = lanes_of()
    gx = lax.axis_index("gx")
    even = lax.rem(gx, 2) == 0
    west_in = (gx > 0).astype(F32)
    east_in = (gx < 7).astype(F32)

    def bring(d, _):
        for f in range(12):
            at = pl.multiple_of((d * 12 + f) * 24, 8)
            from_a = recv_a[pl.ds(at, 24), :]
            from_b = recv_b[pl.ds(at, 24), :]
            west = jnp.where(even, from_b, from_a)
            east = jnp.where(even, from_a, from_b)
            if f < NC:
                iters[d, f] = west
                iters[8 + EARLY + d, f] = east
            else:
                perms[d, f - 9] = west * west_in
                perms[8 + EARLY + d, f - 9] = east * east_in
        return 0

    lax.fori_loop(0, EARLY, bring, 0)

    def bring_ratio(d, _):
        for c in range(NC):
            at = pl.multiple_of(RATIO_AT + (d * NC + c) * 16, 8)
            from_a = recv_a[pl.ds(at, 16), :]
            from_b = recv_b[pl.ds(at, 16), :]
            ratios[d, c] = jnp.where(even, from_b, from_a)
            ratios[LATE + d, c] = jnp.where(even, from_a, from_b)
        return 0

    lax.fori_loop(0, LATE, bring_ratio, 0)

    def settle(x, _):
        for f in range(NC):
            iters[EARLY + x, f] = wide[x, f]
        for f in range(3):
            perms[EARLY + x, f] = wide[x, 9 + f]
        return 0

    lax.fori_loop(0, 8, settle, 0)

    def column(at, ratio_of):
        here = at + 1

        def three(ref, *index):
            return tuple(ref[index + (slice(8 * t, 8 * t + 8), slice(None))] for t in range(3))

        px = three(perms, here, 0)
        py = three(perms, here, 1)
        pz = three(perms, here, 2)
        t_east = [a * b for a, b in zip(px, three(perms, here + 1, 0))]
        t_west = [a * b for a, b in zip(px, three(perms, here - 1, 0))]
        t_north = [a * b for a, b in zip(py, north_of(py, row))]
        t_south = [a * b for a, b in zip(py, south_of(py, row))]
        t_up = [jnp.where(lane < 127, a * pltpu.roll(a, 127, 1), 0.0) for a in pz]
        t_down = [jnp.where(lane > 0, a * pltpu.roll(a, 1, 1), 0.0) for a in pz]
        kinds = (t_east, t_west, t_north, t_south, t_up, t_down)
        total = [sum(kind[t] for kind in kinds) for t in range(3)]

        def outer(tiles):
            return jnp.where(row < 4, tiles[2], tiles[0])

        def edge(tiles):
            return jnp.where(row == 4, tiles[2], tiles[0])

        for n, kind in enumerate(kinds):
            trans[at, n, 0:8, :] = kind[1]
            trans[at, n, 8:16, :] = outer(kind)
        for c in range(NC):
            mid = three(iters, here, c)
            east = three(iters, here + 1, c)
            west = three(iters, here - 1, c)
            north = north_of(mid, row)
            south = south_of(mid, row)
            beside = []
            for t in range(3):
                value = t_east[t] * east[t] + t_west[t] * west[t]
                value = value + t_north[t] * north[t] + t_south[t] * south[t]
                value = value + t_up[t] * pltpu.roll(mid[t], 127, 1)
                value = value + t_down[t] * pltpu.roll(mid[t], 1, 1)
                beside.append(value)
            ratio = ratio_of(c)
            scale = OMEGA / (ratio[0] + total[1])
            gain[at, c, 0:8, :] = scale
            begin[at, c, 0:8, :] = KEEP * mid[1] + scale * beside[1]
            scale = OMEGA / (ratio[1] + outer(total))
            gain[at, c, 8:16, :] = scale
            begin[at, c, 8:16, :] = KEEP * outer(mid) + scale * outer(beside)
            if ratio[2] is not None:
                scale = OMEGA / (ratio[2] + edge(total))
                begin_edge[at - LATE, c] = KEEP * edge(mid) + scale * edge(beside)

    def home_column(x, _):
        def ratio_of(c):
            south = wide[x, 12 + c, 0:8, :]
            north = wide[x, 12 + c, 16:24, :]
            return (
                wide[x, 12 + c, 8:16, :],
                jnp.where(row < 4, north, south),
                jnp.where(row == 4, north, south),
            )

        column(x + LATE, ratio_of)
        return 0

    def halo_column(d, _):
        def ratio_of(c):
            return (ratios[d, c, 0:8, :], ratios[d, c, 8:16, :], None)

        column(jnp.where(d < LATE, d, d + 8), ratio_of)
        return 0

    lax.fori_loop(0, 8, home_column, 0)
    lax.fori_loop(0, 2 * LATE, halo_column, 0)


def scatter_kernel(
    cell, arrived, wide, recv_a, recv_b, cot, accum, mobil, weight, send_a, send_b, left, right, total
):
    row = rows_of()
    lane = lanes_of()
    row16 = rows_of((16, 128))
    gx = lax.axis_index("gx")
    even_x = lax.rem(gx, 2) == 0

    def build(j, _):
        for half in range(2):
            at = pl.ds(pl.multiple_of(j * 256 + half * 128, 128), 128)
            place = cell[j, half : half + 1, :]
            place = jnp.broadcast_to(place, (16, 128))
            low = lax.bitwise_and(lax.shift_right_logical(place, 7), 15)
            high = lax.bitwise_or(
                lax.bitwise_and(place, 127),
                lax.shift_left(lax.shift_right_logical(place, 11), 7),
            )
            mine = low == row16
            values = arrived[j, pl.ds(half, NC, stride=2), :]
            coarse = values.astype(BF16).astype(F32)
            fine = values - coarse
            for c in range(NC):
                for part, source in ((0, coarse), (1, fine)):
                    line = jnp.broadcast_to(source[c : c + 1, :], (16, 128))
                    left[part * 144 + c * 16 : part * 144 + c * 16 + 16, at] = jnp.where(
                        mine, line, 0.0
                    ).astype(BF16)
            for n in range(32):
                right[n * 16 : n * 16 + 16, at] = jnp.where(
                    high == row16 + n * 16, 1.0, 0.0
                ).astype(BF16)
        return 0

    lax.fori_loop(0, BRICKS, build, 0)

    west_in = (gx > 0).astype(F32)
    east_in = (gx < 7).astype(F32)
    at_west = slice(((EARLY - 1) * 12 + 9) * 24 + 8, ((EARLY - 1) * 12 + 9) * 24 + 16)
    at_east = slice(9 * 24 + 8, 9 * 24 + 16)
    px_west = jnp.where(even_x, recv_b[at_west, :], recv_a[at_west, :]) * west_in
    px_east = jnp.where(even_x, recv_a[at_east, :], recv_b[at_east, :]) * east_in
    for x in range(8):
        px = wide[x, 9, 8:16, :]
        east = wide[x + 1, 9, 8:16, :] if x < 7 else px_east
        west = wide[x - 1, 9, 8:16, :] if x > 0 else px_west
        value = px * east + px * west
        py = tuple(wide[x, 10, 8 * t : 8 * t + 8, :] for t in range(3))
        value = value + py[1] * north_of(py, row)[1] + py[1] * south_of(py, row)[1]
        pz = wide[x, 11, 8:16, :]
        value = value + jnp.where(lane < 127, pz * pltpu.roll(pz, 127, 1), 0.0)
        value = value + jnp.where(lane > 0, pz * pltpu.roll(pz, 1, 1), 0.0)
        total[x * 8 : x * 8 + 8, :] = value

    for part in range(2):
        product = lax.dot_general(
            left[...],
            right[part * 256 : part * 256 + 256, :],
            (((1,), (1,)), ((), ())),
            preferred_element_type=F32,
        )
        for side in range(2):
            pair = part * 2 + side
            at = slice(side * 128, side * 128 + 128)
            for c in range(NC):
                well = product[c * 16 : c * 16 + 16, at] + product[144 + c * 16 : 160 + c * 16, at]
                here = slice((c * 4 + pair) * 16, (c * 4 + pair) * 16 + 16)
                diagonal = accum[here, :].astype(F32) + mobil[here, :].astype(F32) * total[
                    pair * 16 : pair * 16 + 16, :
                ]
                weight[here, :] = OMEGA * (cot[here, :].astype(F32) - well) / diagonal

    even = lax.rem(lax.axis_index("gy"), 2) == 0
    for buffer in (send_a, send_b):
        buffer[0:8, :] = jnp.zeros(TILE, F32)
        buffer[LATE_ROWS - 8 : LATE_ROWS, :] = jnp.zeros(TILE, F32)
    for i in range(NC * 8):
        low = weight[i * 8 : i * 8 + LATE, :]
        high = weight[i * 8 + 8 - LATE : i * 8 + 8, :]
        at = slice(8 + i * LATE, 8 + i * LATE + LATE)
        send_a[at, :] = jnp.where(even, high, low)
        send_b[at, :] = jnp.where(even, low, high)


def late_wide_kernel(weight, recv_a, recv_b, wide, edge, send_a, send_b):
    row = rows_of()
    even = lax.rem(lax.axis_index("gy"), 2) == 0
    for c in range(NC):
        for x in range(8):
            i = c * 8 + x
            at = 8 + i * LATE
            low = slice(at - (8 - LATE), at + LATE)
            high = slice(at, at + 8)
            south = jnp.where(even, recv_b[low, :], recv_a[low, :])
            north = jnp.where(even, recv_a[high, :], recv_b[high, :])
            wide[x, c, 0:8, :] = weight[i * 8 : i * 8 + 8, :]
            wide[x, c, 8:16, :] = jnp.where(row < 4, north, south)
            edge[x, c] = jnp.where(row == 4, north, south)
    even_x = lax.rem(lax.axis_index("gx"), 2) == 0
    for buffer, east in ((send_a, even_x), (send_b, jnp.logical_not(even_x))):
        first = jnp.where(east, 8 - LATE, 0)
        for d in range(LATE):
            for c in range(NC):
                buffer[d, c] = wide[first + d, c]


def sweep_kernel(
    trans, gain, begin, begin_edge, wide, edge, recv_a, recv_b, result, weight, one, two
):
    row = rows_of()
    even = lax.rem(lax.axis_index("gx"), 2) == 0

    def bring(d, _):
        for c in range(NC):
            from_a = recv_a[d, c]
            from_b = recv_b[d, c]
            west = jnp.where(even, from_b, from_a)
            east = jnp.where(even, from_a, from_b)
            weight[d, c] = west
            weight[8 + LATE + d, c] = east
            one[d, c] = west + begin[d, c]
            one[8 + LATE + d, c] = east + begin[8 + LATE + d, c]
        return 0

    lax.fori_loop(0, LATE, bring, 0)

    def settle(x, _):
        for c in range(NC):
            weight[LATE + x, c] = wide[x, c]
            one[LATE + x, c] = wide[x, c] + begin[LATE + x, c]
        return 0

    lax.fori_loop(0, 8, settle, 0)
    first = row == 0
    last = row == 7

    def column(at, held, new, brim, final):
        kinds = [[trans[at, n, 8 * t : 8 * t + 8, :] for t in range(2)] for n in range(6)]
        t_east, t_west, t_north, t_south, t_up, t_down = kinds
        for c in range(NC):
            mid = [held[at, c, 8 * t : 8 * t + 8, :] for t in range(2)]
            east = [held[at + 1, c, 8 * t : 8 * t + 8, :] for t in range(2)]
            west = [held[at - 1, c, 8 * t : 8 * t + 8, :] for t in range(2)]
            back = [pltpu.roll(tile, 7, 0) for tile in mid]
            fore = [pltpu.roll(tile, 1, 0) for tile in mid]
            north = [jnp.where(last, back[1], back[0]), jnp.where(last, back[0], back[1])]
            south = [jnp.where(first, fore[1], fore[0]), jnp.where(first, fore[0], fore[1])]
            if brim:
                outer = begin_edge[at - LATE, c] + edge[at - LATE, c]
                north[1] = jnp.where(row == 3, pltpu.roll(outer, 7, 0), north[1])
                south[1] = jnp.where(row == 4, pltpu.roll(outer, 1, 0), south[1])
            for t in range(1 if final else 2):
                value = t_east[t] * east[t] + t_west[t] * west[t]
                value = value + t_north[t] * north[t] + t_south[t] * south[t]
                value = value + t_up[t] * pltpu.roll(mid[t], 127, 1)
                value = value + t_down[t] * pltpu.roll(mid[t], 1, 1)
                part = slice(8 * t, 8 * t + 8)
                value = KEEP * mid[t] + weight[at, c, part, :] + gain[at, c, part, :] * value
                if final:
                    result[c, at - LATE] = value
                else:
                    new[at, c, part, :] = value

    def sweep(begin_at, end_at, held, new, brim=False, final=False):
        def body(at, _):
            column(at, held, new, brim, final)
            return 0

        lax.fori_loop(begin_at, end_at, body, 0)

    sweep(1, LATE, one, two)
    sweep(LATE, LATE + 8, one, two, brim=True)
    sweep(LATE + 8, COLS - 1, one, two)
    sweep(2, COLS - 2, two, one)
    sweep(3, COLS - 3, one, two)
    sweep(4, COLS - 4, two, one)
    sweep(5, COLS - 5, one, None, final=True)


def swap_pairs(shards, axis):
    count = lax.axis_size(axis)
    inner = [(i, i ^ 1) for i in range(count)]
    outer = [(i, (((i + 1) ^ 1) - 1) % count) for i in range(count)]
    return lax.ppermute(shards[0], axis, inner), lax.ppermute(shards[1], axis, outer)


def body(
    seg_source,
    seg_inverse,
    seg_outflow,
    well_len,
    perf_seg,
    perf_count,
    perf_coupling,
    recv_cell,
    cell_cot,
    start_iterate,
    accumulation,
    mobility,
    perm_x,
    perm_y,
    perm_z,
):
    cot = cell_cot.reshape(NC * 64, 128)
    accum = accumulation.reshape(NC * 64, 128)
    mobil = mobility.reshape(NC * 64, 128)
    ratio, early_a, early_b = call(
        early_pack_kernel,
        (out(NC * 64, 128), out(EARLY_ROWS, 128), out(EARLY_ROWS, 128)),
        [],
        [VMEM] * 6,
        "early_pack",
    )(start_iterate, perm_x, perm_y, perm_z, accum, mobil)
    early_a, early_b = swap_pairs((early_a, early_b), "gy")

    mats, vecs, head = call(
        scan_kernel,
        (out(81, 8, 128), out(NC, 8, 128), out(BRICKS, 8, 128)),
        [pltpu.VMEM((90, 8, 128), F32)],
        [SMEM, VMEM, VMEM, VMEM],
        "well_scan",
        10_000_000,
    )(well_len, seg_source, seg_inverse, seg_outflow)
    heads = lax.all_to_all(head, "gy", 0, 0, tiled=True)

    wide, wide_a, wide_b = call(
        early_wide_kernel,
        (out(8, FIELDS, 24, 128), out(WIDE_ROWS, 128), out(WIDE_ROWS, 128)),
        [],
        [VMEM] * 7,
        "early_wide",
    )(start_iterate, perm_x, perm_y, perm_z, ratio, early_a, early_b)
    wide_a, wide_b = swap_pairs((wide_a, wide_b), "gx")

    lam, sent = call(
        rows_kernel,
        (out(NC, 8, 128), out(BRICKS * SLOT, 128)),
        [],
        [SMEM] + [VMEM] * 5,
        "well_rows",
    )(
        perf_count.reshape(BRICKS),
        mats,
        vecs,
        heads,
        perf_seg.reshape(BRICKS, 256),
        perf_coupling.reshape(NC, NC, BRICKS, 256),
    )
    arrived = lax.all_to_all(sent, "gy", 0, 0, tiled=True)

    weight, late_a, late_b = call(
        scatter_kernel,
        (out(NC * 64, 128), out(LATE_ROWS, 128), out(LATE_ROWS, 128)),
        [
            pltpu.VMEM((288, 4096), BF16),
            pltpu.VMEM((512, 4096), BF16),
            pltpu.VMEM((64, 128), F32),
        ],
        [VMEM] * 8,
        "scatter",
        limit=32,
    )(recv_cell.reshape(BRICKS, 2, 128), arrived.reshape(BRICKS, SLOT, 128), wide, wide_a, wide_b, cot, accum, mobil)
    late_a, late_b = swap_pairs((late_a, late_b), "gy")

    trans, gain, begin, begin_edge = call(
        early_kernel,
        (
            out(COLS, 6, 16, 128),
            out(COLS, NC, 16, 128),
            out(COLS, NC, 16, 128),
            out(8, NC, 8, 128),
        ),
        [
            pltpu.VMEM((8 + 2 * EARLY, NC, 24, 128), F32),
            pltpu.VMEM((8 + 2 * EARLY, 3, 24, 128), F32),
            pltpu.VMEM((2 * LATE, NC, 16, 128), F32),
        ],
        [VMEM] * 3,
        "early",
        limit=24,
    )(wide, wide_a, wide_b)

    widened, edge, side_a, side_b = call(
        late_wide_kernel,
        (
            out(8, NC, 16, 128),
            out(8, NC, 8, 128),
            out(LATE, NC, 16, 128),
            out(LATE, NC, 16, 128),
        ),
        [],
        [VMEM] * 3,
        "late_wide",
    )(weight, late_a, late_b)
    side_a, side_b = swap_pairs((side_a, side_b), "gx")

    wide_field = pltpu.VMEM((COLS, NC, 16, 128), F32)
    result = call(
        sweep_kernel,
        out(NC, 8, 8, 128),
        [wide_field] * 3,
        [VMEM] * 8,
        "sweeps",
        limit=24,
    )(trans, gain, begin, begin_edge, widened, edge, side_a, side_b)
    return lam, result


def solution(mesh):
    return jax.shard_map(
        body,
        mesh=mesh,
        in_specs=(
            P(None, "gx", "gy"),
            P(None, None, "gx", "gy"),
            P(None, None, "gx", "gy"),
            P("gx"),
            P("gx", "gy", None, None),
            P("gx", "gy", None),
            P(None, None, "gx", "gy", None, None),
            P("gx", "gy", None, None),
            P(None, "gx", "gy", None),
            P(None, "gx", "gy", None),
            P(None, "gx", "gy", None),
            P(None, "gx", "gy", None),
            P("gx", "gy", None),
            P("gx", "gy", None),
            P("gx", "gy", None),
        ),
        out_specs=(P(None, "gx", "gy"), P(None, "gx", "gy", None)),
        check_vma=False,
    )
```

profile of v0, /device:TPU:0, one launch (start us, length us, event | category | flops | bytes accessed | tf_op | source)
XLA Modules:
  0.0 97.9 jit_solution(17803045191467093877)
XLA Ops:
  0.7 1.0 copy-done.1
  1.6 0.9 copy-done.2
  2.5 0.9 copy-done.4
  3.4 0.8 copy-done.10
  4.2 0.8 copy-done.11
  5.0 0.8 copy-done.12
  5.7 0.2 early_pack.1
  5.9 1.7 %collective-permute-start = (f32[1024,128]{1,0:T(8,128)S(1)}, f32[1024,128]{1,0:T(8,128)S(1)}, u32[]{:S(2)}, u32[]{:S(2)}) collective-permute-start(f32[1024,128]{1,0:T(8,128)S(1)} %get-tuple-element.29), channel_id=1, source_target_pairs={{0,1},{1,0},{2,3},{3,2},{4,5},{5,4},{6,7},{7,6},{8,9},{9,8},{10,11... | collective-permute-start | bytes 1572872 | tf_op jit(solution)/shard_map/ppermute | solution.py:550
  7.6 4.5 %collective-permute-start.1 = (f32[1024,128]{1,0:T(8,128)S(1)}, f32[1024,128]{1,0:T(8,128)S(1)}, u32[]{:S(2)}, u32[]{:S(2)}) collective-permute-start(f32[1024,128]{1,0:T(8,128)S(1)} %get-tuple-element.30), channel_id=1, source_target_pairs={{0,15},{1,2},{2,1},{3,4},{4,3},{5,6},{6,5},{7,8},{8,7},{9,10},{10,... | collective-permute-start | bytes 1572872 | tf_op jit(solution)/shard_map/ppermute | solution.py:550
  12.1 7.4 %collective-permute-done.recv_a = f32[1024,128]{1,0:T(8,128)S(1)} collective-permute-done((f32[1024,128]{1,0:T(8,128)S(1)}, f32[1024,128]{1,0:T(8,128)S(1)}, u32[]{:S(2)}, u32[]{:S(2)}) %collective-permute-start) | collective-permute-done | bytes 524320 | tf_op jit(solution)/shard_map/ppermute | solution.py:550
  19.5 4.8 %collective-permute-done.1.recv_b = f32[1024,128]{1,0:T(8,128)S(1)} collective-permute-done((f32[1024,128]{1,0:T(8,128)S(1)}, f32[1024,128]{1,0:T(8,128)S(1)}, u32[]{:S(2)}, u32[]{:S(2)}) %collective-permute-start.1) | collective-permute-done | bytes 524320 | tf_op jit(solution)/shard_map/ppermute | solution.py:550
  24.3 1.9 %early_wide.1 = (f32[8,21,24,128]{3,2,1,0:T(8,128)S(1)}, f32[2448,128]{1,0:T(8,128)}, f32[2448,128]{1,0:T(8,128)}) custom-call(f32[9,8,8,128]{3,2,1,0:T(8,128)S(1)} %copy-done.1, f32[8,8,128]{2,1,0:T(8,128)S(1)} %copy-done.10, f32[8,8,128]{2,1,0:T(8,128)S(1)} %copy-done.11, f32[8,8,128]{2,1,0:T(8,128)S(1)} %copy-done.12, ...), custom_call_target="tpu_custom_call" | custom-call | flops 1000000 | bytes 1000000 | tf_op jit(solution)/shard_map/early_wide/pallas_call | solution.py:592
  26.1 4.1 %collective-permute-start.3 = (f32[2448,128]{1,0:T(8,128)}, f32[2448,128]{1,0:T(8,128)}, u32[]{:S(2)}, u32[]{:S(2)}) collective-permute-start(f32[2448,128]{1,0:T(8,128)} %get-tuple-element.33), channel_id=1, source_target_pairs={{0,112},{16,32},{32,16},{48,64},{64,48},{80,96},{96,80},{112,0},{1... | collective-permute-start | bytes 3760136 | tf_op jit(solution)/shard_map/ppermute | solution.py:550
  30.3 3.8 %well_scan.1 = (f32[81,8,128]{2,1,0:T(8,128)S(1)}, f32[9,8,128]{2,1,0:T(8,128)S(1)}, f32[16,8,128]{2,1,0:T(8,128)S(1)}) custom-call(s32[8]{0:T(128)S(1)} %copy-done.15, f32[9,8,128]{2,1,0:T(8,128)S(1)} %copy-done.13, f32[9,9,8,128]{3,2,1,0:T(8,128)S(1)} %copy-done.6, f32[9,9,8,128]{3,2,1,0:T(8,128)S(1)} %copy-done.7), custom_call_target="tpu_custom_call" | custom-call | flops 10000000 | bytes 1000000 | tf_op jit(solution)/shard_map/well_scan/pallas_call | solution.py:582
  34.1 13.4 %all_to_all.14.heads = f32[16,8,128]{2,1,0:T(8,128)S(1)} all-to-all(f32[16,8,128]{2,1,0:T(8,128)S(1)} %get-tuple-element.26), channel_id=1, replica_groups=mesh['gx'=8,'gy'=16] {'gy'}, dimensions={0} | all-to-all | bytes 131072 | tf_op jit(solution)/shard_map/all_to_all | solution.py:590
  47.5 4.7 %well_rows.1 = (f32[9,8,128]{2,1,0:T(8,128)}, f32[384,128]{1,0:T(8,128)S(1)}) custom-call(s32[16]{0:T(128)S(1)} %bitcast.17, f32[81,8,128]{2,1,0:T(8,128)S(1)} %get-tuple-element.24.mats, f32[9,8,128]{2,1,0:T(8,128)S(1)} %get-tuple-element.25.vecs, f32[16,8,128]{2,1,0:T(8,128)S(1)} %all_to_all.14.heads, s32[16,256]{1,0:T(8,128)S(1)} %bitcast.16, ...), custom_call_target="tpu_custom_call" | custom-call | flops 1000000 | bytes 1000000 | tf_op jit(solution)/shard_map/well_rows/pallas_call | solution.py:601
  52.2 0.7 copy-done.8
  52.9 3.5 %all-to-all-start.1 = ((f32[16,24,128]{2,1,0:T(8,128)}), f32[16,24,128]{2,1,0:T(8,128)S(1)}, u32[]{:S(2)}, u32[]{:S(2)}) async-start(f32[16,24,128]{2,1,0:T(8,128)} %bitcast.14), calls=%async_computation.1 | async-start | bytes 393216 | tf_op jit(solution)/shard_map/all_to_all | solution.py:615
  56.4 8.3 %all-to-all-done.1.arrived = f32[16,24,128]{2,1,0:T(8,128)S(1)} async-done(((f32[16,24,128]{2,1,0:T(8,128)}), f32[16,24,128]{2,1,0:T(8,128)S(1)}, u32[]{:S(2)}, u32[]{:S(2)}) %all-to-all-start.1) | async-done | bytes 196640 | tf_op jit(solution)/shard_map/all_to_all | solution.py:615
  64.7 0.9 copy-done.3
  65.6 0.9 copy-done.5
  66.5 0.9 copy-done.9
  67.4 4.9 %scatter.1 = (f32[576,128]{1,0:T(8,128)S(1)}, f32[376,128]{1,0:T(8,128)S(1)}, f32[376,128]{1,0:T(8,128)S(1)}) custom-call(s32[16,2,128]{2,1,0:T(2,128)S(1)} %reshape.34.cell, f32[16,24,128]{2,1,0:T(8,128)S(1)} %all-to-all-done.1.arrived, f32[8,21,24,128]{3,2,1,0:T(8,128)S(1)} %get-tuple-element.31.wide, f32[2448,128]{1,0:T(8,128)S(1)} %collective-permute-done.2.recv_a, ...), custom_call_target="tpu_custom_call" | custom-call | flops 1000000 | bytes 1000000 | tf_op jit(solution)/shard_map/scatter/pallas_call | solution.py:617
  72.4 0.7 collective-permute-start.4
  73.0 1.6 %collective-permute-start.5 = (f32[376,128]{1,0:T(8,128)S(1)}, f32[376,128]{1,0:T(8,128)S(1)}, u32[]{:S(2)}, u32[]{:S(2)}) collective-permute-start(f32[376,128]{1,0:T(8,128)S(1)} %get-tuple-element.41), channel_id=1, source_target_pairs={{0,15},{1,2},{2,1},{3,4},{4,3},{5,6},{6,5},{7,8},{8,7},{9,10},{10,... | collective-permute-start | bytes 577544 | tf_op jit(solution)/shard_map/ppermute | solution.py:550
  74.6 3.4 %collective-permute-done.4.recv_a = f32[376,128]{1,0:T(8,128)S(1)} collective-permute-done((f32[376,128]{1,0:T(8,128)S(1)}, f32[376,128]{1,0:T(8,128)S(1)}, u32[]{:S(2)}, u32[]{:S(2)}) %collective-permute-start.4) | collective-permute-done | bytes 192544 | tf_op jit(solution)/shard_map/ppermute | solution.py:550
  78.1 3.9 %collective-permute-done.5.recv_b = f32[376,128]{1,0:T(8,128)S(1)} collective-permute-done((f32[376,128]{1,0:T(8,128)S(1)}, f32[376,128]{1,0:T(8,128)S(1)}, u32[]{:S(2)}, u32[]{:S(2)}) %collective-permute-start.5) | collective-permute-done | bytes 192544 | tf_op jit(solution)/shard_map/ppermute | solution.py:550
  82.0 0.2 late_wide.1
  82.2 0.5 collective-permute-start.7
  82.7 4.0 %early.1 = (f32[18,6,16,128]{3,2,1,0:T(8,128)S(1)}, f32[18,9,16,128]{3,2,1,0:T(8,128)S(1)}, f32[18,9,16,128]{3,2,1,0:T(8,128)S(1)}, f32[8,9,8,128]{3,2,1,0:T(8,128)S(1)}) custom-call(f32[8,21,24,128]{3,2,1,0:T(8,128)S(1)} %get-tuple-element.31.wide, f32[2448,128]{1,0:T(8,128)S(1)} %collective-permute-done.2.recv_a, f32[2448,128]{1,0:T(8,128)} %collective-permute-done.3.recv_b), custom_call_target="tpu_custom_call" | custom-call | flops 1000000 | bytes 1000000 | tf_op jit(solution)/shard_map/early/pallas_call | solution.py:631
  86.8 3.7 %collective-permute-done.7.recv_b = f32[5,9,16,128]{3,2,1,0:T(8,128)S(1)} collective-permute-done((f32[5,9,16,128]{3,2,1,0:T(8,128)S(1)}, f32[5,9,16,128]{3,2,1,0:T(8,128)S(1)}, u32[]{:S(2)}, u32[]{:S(2)}) %collective-permute-start.7) | collective-permute-done | bytes 368672 | tf_op jit(solution)/shard_map/ppermute | solution.py:550
  90.5 7.5 %sweeps.1 = f32[9,8,8,128]{3,2,1,0:T(8,128)} custom-call(f32[18,6,16,128]{3,2,1,0:T(8,128)S(1)} %get-tuple-element.34.trans, f32[18,9,16,128]{3,2,1,0:T(8,128)S(1)} %get-tuple-element.35.gain, f32[18,9,16,128]{3,2,1,0:T(8,128)S(1)} %get-tuple-element.36.begin, f32[8,9,8,128]{3,2,1,0:T(8,128)S(1)} %get-tuple-element.37.begin_edge, ...), custom_call_target="tpu_custom_call" | custom-call | flops 1000000 | bytes 1000000 | tf_op jit(solution)/shard_map/sweeps/pallas_call | solution.py:664
  (32 shorter events, 0.2 us)
Async XLA Ops:
  0.6 29.7 %copy-start.15 = (s32[8]{0:T(128)S(1)}, s32[8]{0:T(128)}, u32[]{:S(2)}) copy-start(s32[8]{0:T(128)} %len_ref.1) | copy-start | bytes 100
  0.6 1.0 copy-start.1
  1.6 0.9 copy-start.2
  2.5 0.9 copy-start.4
  3.4 0.8 copy-start.10
  4.2 0.8 copy-start.11
  4.9 0.8 copy-start.12
  5.7 24.6 %copy-start.6 = (f32[9,9,8,128]{3,2,1,0:T(8,128)S(1)}, f32[9,9,8,128]{3,2,1,0:T(8,128)}, u32[]{:S(2)}) copy-start(f32[9,9,8,128]{3,2,1,0:T(8,128)} %inv.1) | copy-start | bytes 995332
  5.7 24.6 %copy-start.7 = (f32[9,9,8,128]{3,2,1,0:T(8,128)S(1)}, f32[9,9,8,128]{3,2,1,0:T(8,128)}, u32[]{:S(2)}) copy-start(f32[9,9,8,128]{3,2,1,0:T(8,128)} %outf.1) | copy-start | bytes 995332
  5.7 24.6 %copy-start.13 = (f32[9,8,128]{2,1,0:T(8,128)S(1)}, f32[9,8,128]{2,1,0:T(8,128)}, u32[]{:S(2)}) copy-start(f32[9,8,128]{2,1,0:T(8,128)} %src.1) | copy-start | bytes 110596
  5.9 41.6 %copy-start = (f32[9,9,1,1,16,256]{5,4,3,2,1,0:T(8,128)S(1)}, f32[9,9,1,1,16,256]{5,4,3,2,1,0:T(8,128)}, u32[]{:S(2)}) copy-start(f32[9,9,1,1,16,256]{5,4,3,2,1,0:T(8,128)} %param.21) | copy-start | bytes 3981316
  5.9 41.6 %copy-start.14 = (s32[1,1,16,256]{3,2,1,0:T(8,128)S(1)}, s32[1,1,16,256]{3,2,1,0:T(8,128)}, u32[]{:S(2)}) copy-start(s32[1,1,16,256]{3,2,1,0:T(8,128)} %param.19) | copy-start | bytes 49156
  5.9 41.6 %copy-start.16 = (s32[1,1,16]{2,1,0:T(1,128)S(1)}, s32[1,1,16]{2,1,0:T(1,128)}, u32[]{:S(2)}) copy-start(s32[1,1,16]{2,1,0:T(1,128)} %param.20) | copy-start | bytes 196
  5.9 13.6 %collective-permute-start = (f32[1024,128]{1,0:T(8,128)S(1)}, f32[1024,128]{1,0:T(8,128)S(1)}, u32[]{:S(2)}, u32[]{:S(2)}) collective-permute-start(f32[1024,128]{1,0:T(8,128)S(1)} %get-tuple-element.29), channel_id=1, source_target_pairs={{0,1},{1,0},{2,3},{3,2},{4,5},{5,4},{6,7},{7,6},{8,9},{9,8},{10,11... | collective-permute-start | bytes 1572872 | tf_op jit(solution)/shard_map/ppermute | solution.py:550
  7.6 16.7 %collective-permute-start.1 = (f32[1024,128]{1,0:T(8,128)S(1)}, f32[1024,128]{1,0:T(8,128)S(1)}, u32[]{:S(2)}, u32[]{:S(2)}) collective-permute-start(f32[1024,128]{1,0:T(8,128)S(1)} %get-tuple-element.30), channel_id=1, source_target_pairs={{0,15},{1,2},{2,1},{3,4},{4,3},{5,6},{6,5},{7,8},{8,7},{9,10},{10,... | collective-permute-start | bytes 1572872 | tf_op jit(solution)/shard_map/ppermute | solution.py:550
  26.1 38.6 %collective-permute-start.2 = (f32[2448,128]{1,0:T(8,128)}, f32[2448,128]{1,0:T(8,128)S(1)}, u32[]{:S(2)}, u32[]{:S(2)}) collective-permute-start(f32[2448,128]{1,0:T(8,128)} %get-tuple-element.32), channel_id=1, source_target_pairs={{0,16},{16,0},{32,48},{48,32},{64,80},{80,64},{96,112},{112,96},{1... | collective-permute-start | bytes 3760136 | tf_op jit(solution)/shard_map/ppermute | solution.py:550
  26.1 38.6 %collective-permute-start.3 = (f32[2448,128]{1,0:T(8,128)}, f32[2448,128]{1,0:T(8,128)}, u32[]{:S(2)}, u32[]{:S(2)}) collective-permute-start(f32[2448,128]{1,0:T(8,128)} %get-tuple-element.33), channel_id=1, source_target_pairs={{0,112},{16,32},{32,16},{48,64},{64,48},{80,96},{96,80},{112,0},{1... | collective-permute-start | bytes 3760136 | tf_op jit(solution)/shard_map/ppermute | solution.py:550
  34.1 22.3 %copy-start.17 = (s32[1,1,16,256]{3,2,1,0:T(8,128)S(1)}, s32[1,1,16,256]{3,2,1,0:T(8,128)}, u32[]{:S(2)}) copy-start(s32[1,1,16,256]{3,2,1,0:T(8,128)} %param.22) | copy-start | bytes 49156
  52.2 0.7 copy-start.8
  52.9 11.8 %all-to-all-start.1 = ((f32[16,24,128]{2,1,0:T(8,128)}), f32[16,24,128]{2,1,0:T(8,128)S(1)}, u32[]{:S(2)}, u32[]{:S(2)}) async-start(f32[16,24,128]{2,1,0:T(8,128)} %bitcast.14), calls=%async_computation.1 | async-start | bytes 393216 | tf_op jit(solution)/shard_map/all_to_all | solution.py:615
  64.7 0.9 copy-start.3
  65.6 0.9 copy-start.5
  66.5 0.9 copy-start.9
  72.4 5.7 %collective-permute-start.4 = (f32[376,128]{1,0:T(8,128)S(1)}, f32[376,128]{1,0:T(8,128)S(1)}, u32[]{:S(2)}, u32[]{:S(2)}) collective-permute-start(f32[376,128]{1,0:T(8,128)S(1)} %get-tuple-element.40), channel_id=1, source_target_pairs={{0,1},{1,0},{2,3},{3,2},{4,5},{5,4},{6,7},{7,6},{8,9},{9,8},{10,11... | collective-permute-start | bytes 577544 | tf_op jit(solution)/shard_map/ppermute | solution.py:550
  73.0 8.9 %collective-permute-start.5 = (f32[376,128]{1,0:T(8,128)S(1)}, f32[376,128]{1,0:T(8,128)S(1)}, u32[]{:S(2)}, u32[]{:S(2)}) collective-permute-start(f32[376,128]{1,0:T(8,128)S(1)} %get-tuple-element.41), channel_id=1, source_target_pairs={{0,15},{1,2},{2,1},{3,4},{4,3},{5,6},{6,5},{7,8},{8,7},{9,10},{10,... | collective-permute-start | bytes 577544 | tf_op jit(solution)/shard_map/ppermute | solution.py:550
  82.1 4.6 %collective-permute-start.6 = (f32[5,9,16,128]{3,2,1,0:T(8,128)S(1)}, f32[5,9,16,128]{3,2,1,0:T(8,128)S(1)}, u32[]{:S(2)}, u32[]{:S(2)}) collective-permute-start(f32[5,9,16,128]{3,2,1,0:T(8,128)S(1)} %get-tuple-element.44), channel_id=1, source_target_pairs={{0,16},{16,0},{32,48},{48,32},{64,80},{80,64},{96,112},{112,96},{1... | collective-permute-start | bytes 1105928 | tf_op jit(solution)/shard_map/ppermute | solution.py:550
  82.2 8.2 %collective-permute-start.7 = (f32[5,9,16,128]{3,2,1,0:T(8,128)S(1)}, f32[5,9,16,128]{3,2,1,0:T(8,128)S(1)}, u32[]{:S(2)}, u32[]{:S(2)}) collective-permute-start(f32[5,9,16,128]{3,2,1,0:T(8,128)S(1)} %get-tuple-element.45), channel_id=1, source_target_pairs={{0,112},{16,32},{32,16},{48,64},{64,48},{80,96},{96,80},{112,0},{1... | collective-permute-start | bytes 1105928 | tf_op jit(solution)/shard_map/ppermute | solution.py:550
where the time goes:
time: 99 us; the launch traced here: 97.9 us
  waiting for transfers between devices  31.4 us (32%)
  Pallas kernels  27.1 us (27%)
  starting transfers between devices  16.7 us (17%)
  blocking collectives  13.4 us (14%)
  local copies, waits for them, and re-layouts  8.51 us (9%)
    all_to_all x1, blocking collectives, body(): heads = lax.all_to_all(head, 'gy', 0, 0, tiled=True)  13.4 us
    ppermute x4, waiting for transfers between devices, swap_pairs(): lax.ppermute(shards[1], axis, outer)  12.3 us
    ppermute x4, waiting for transfers between devices, swap_pairs(): lax.ppermute(shards[0], axis, inner)  10.8 us
    ppermute x4, starting transfers between devices, swap_pairs(): lax.ppermute(shards[1], axis, outer)  10.8 us
    unnamed x36, local copies, waits for them, and re-layouts  8.5 us
    all_to_all x1, waiting for transfers between devices, body(): arrived = lax.all_to_all(sent, 'gy', 0, 0, tiled=True)  8.27 us
    pallas_call x1, Pallas kernels, body(): call(sweep_kernel, out(NC, 8, 8, 128), [wide_field] * 3, [VMEM] * 8, 'swe...  7.48 us
    pallas_call x1, Pallas kernels, body(): call(scatter_kernel, (out(NC * 64, 128), out(LATE_ROWS, 128), out(LATE_RO...  4.93 us
  transfers between devices with their start and end apart: 9, of which 6 were waited for; matrix products, arithmetic and copies ran while one was open for 0% of the time, Pallas kernels for 13%

commit v1 on v0

--- a/solution.py
+++ b/solution.py
@@ -25,6 +25,7 @@
 
 VMEM = pl.BlockSpec(memory_space=pltpu.VMEM)
 SMEM = pl.BlockSpec(memory_space=pltpu.SMEM)
+HBM = pl.BlockSpec(memory_space=pltpu.HBM)
 
 
 def lanes_of(shape=TILE):
@@ -35,12 +36,12 @@
     return lax.broadcasted_iota(I32, shape, 0)
 
 
-def call(kernel, outs, scratch, specs, name, flops=1_000_000, limit=16):
+def call(kernel, outs, scratch, specs, name, flops=1_000_000, limit=8, out_specs=None):
     return pl.pallas_call(
         kernel,
         out_shape=outs,
         in_specs=specs,
-        out_specs=jax.tree.map(lambda _: VMEM, outs),
+        out_specs=jax.tree.map(lambda _: VMEM, outs) if out_specs is None else out_specs,
         scratch_shapes=scratch,
         compiler_params=pltpu.CompilerParams(vmem_limit_bytes=limit * 1024 * 1024),
         cost_estimate=pl.CostEstimate(
@@ -50,11 +51,85 @@
     )
 
 
-def out(*shape):
-    return jax.ShapeDtypeStruct(shape, F32)
-
-
-def scan_kernel(len_ref, src, inv, outf, mats, vecs, head, rolled):
+def out(*shape, dtype=F32):
+    return jax.ShapeDtypeStruct(shape, dtype)
+
+
+def far(*shape, dtype=F32):
+    return pltpu.HBM(shape, dtype)
+
+
+def pin(array):
+    return pltpu.with_memory_space_constraint(array, pltpu.HBM)
+
+
+def fetch(sources, targets, sems):
+    copies = [
+        pltpu.make_async_copy(source, target, sems.at[n])
+        for n, (source, target) in enumerate(zip(sources, targets))
+    ]
+    for copy in copies:
+        copy.start()
+    return copies
+
+
+def first_kernel(
+    len_hbm,
+    src_hbm,
+    inv_hbm,
+    outf_hbm,
+    start_hbm,
+    px_hbm,
+    py_hbm,
+    pz_hbm,
+    accum_hbm,
+    mobil_hbm,
+    mats,
+    vecs,
+    head,
+    ratio,
+    send_a,
+    send_b,
+    edge_a,
+    edge_b,
+    rolled,
+    len_ref,
+    src,
+    inv,
+    outf,
+    start,
+    px,
+    py,
+    pz,
+    accum,
+    mobil,
+    sems,
+):
+    copies = fetch(
+        (
+            inv_hbm,
+            outf_hbm,
+            src_hbm,
+            len_hbm,
+            start_hbm,
+            px_hbm,
+            py_hbm,
+            pz_hbm,
+            accum_hbm,
+            mobil_hbm,
+        ),
+        (inv, outf, src, len_ref, start, px, py, pz, accum, mobil),
+        sems,
+    )
+    for copy in copies[:4]:
+        copy.wait()
+    scan_wells(len_ref, src, inv, outf, mats, vecs, head, rolled)
+    for copy in copies[4:]:
+        copy.wait()
+    early_pack(start, px, py, pz, accum, mobil, ratio, send_a, send_b, edge_a, edge_b)
+
+
+def scan_wells(len_ref, src, inv, outf, mats, vecs, head, rolled):
     lane = lanes_of()
     well = rows_of()
     length = jnp.zeros(TILE, I32)
@@ -113,7 +188,27 @@
         head[j] = packed
 
 
-def rows_kernel(count_ref, mats, vecs, heads, perf_seg, coupling, lam, sent):
+def rows_kernel(
+    count_hbm,
+    seg_hbm,
+    mats,
+    vecs,
+    heads,
+    coupling,
+    edge_a,
+    edge_b,
+    lam_hbm,
+    sent_hbm,
+    token,
+    lam,
+    sent,
+    count_ref,
+    perf_seg,
+    sem,
+    sems,
+    sems_out,
+):
+    copies = fetch((count_hbm, seg_hbm), (count_ref, perf_seg), sems)
     row = rows_of()
     lane = lanes_of()
     me = lax.axis_index("gy")
@@ -136,6 +231,11 @@
         for k in range(NC):
             total = total + mats[c * NC + k] * incoming[k]
         lam[c] = total
+    moves = [pltpu.make_async_copy(lam, lam_hbm, sem)]
+    moves[0].start()
+    token[...] = jnp.zeros(TILE, F32)
+    for copy in copies:
+        copy.wait()
     for block in range(2):
         count = jnp.zeros(TILE, I32)
         for b in range(8):
@@ -161,9 +261,19 @@
                     total = total + coupling[(k, c) + at] * picked[k]
                 total = jnp.where(live, total, 0.0)
                 sent[pl.ds(block * 8 * SLOT + c * 2 + half, 8, stride=SLOT), :] = total
-
-
-def early_pack_kernel(start, px, py, pz, accum, mobil, ratio, send_a, send_b):
+        part = slice(block * 8 * SLOT, block * 8 * SLOT + 8 * SLOT)
+        moves.append(
+            pltpu.make_async_copy(sent.at[part], sent_hbm.at[part], sems_out.at[block])
+        )
+        moves[-1].start()
+    for move in moves:
+        move.wait()
+
+
+def early_pack(start, px, py, pz, accum, mobil, ratio, send_a, send_b, edge_a, edge_b):
+    even_x = lax.rem(lax.axis_index("gx"), 2) == 0
+    edge_a[...] = jnp.where(even_x, px[7], px[0])
+    edge_b[...] = jnp.where(even_x, px[0], px[7])
     even = lax.rem(lax.axis_index("gy"), 2) == 0
     for i in range(NC * 4):
         at = slice(i * 16, i * 16 + 16)
@@ -186,7 +296,47 @@
             send_b[at : at + EARLY, :] = jnp.where(even, low, high)
 
 
-def early_wide_kernel(start, px, py, pz, ratio, recv_a, recv_b, wide, send_a, send_b):
+def shade_kernel(
+    after,
+    start_hbm,
+    px_hbm,
+    py_hbm,
+    pz_hbm,
+    accum_hbm,
+    mobil_hbm,
+    cot_hbm,
+    ratio,
+    recv_a,
+    recv_b,
+    edge_a,
+    edge_b,
+    wide_hbm,
+    send_a_hbm,
+    send_b_hbm,
+    scale_hbm,
+    base_hbm,
+    start,
+    px,
+    py,
+    pz,
+    accum,
+    mobil,
+    cot,
+    wide,
+    send_a,
+    send_b,
+    scale,
+    base,
+    sems,
+    sems_out,
+):
+    copies = fetch(
+        (start_hbm, px_hbm, py_hbm, pz_hbm, accum_hbm, mobil_hbm, cot_hbm),
+        (start, px, py, pz, accum, mobil, cot),
+        sems,
+    )
+    for copy in copies:
+        copy.wait()
     row = rows_of()
     gy = lax.axis_index("gy")
     even = lax.rem(gy, 2) == 0
@@ -207,11 +357,12 @@
                 south = south * south_in
                 north = north * north_in
             else:
-                base = ((f - 12) * 8 + x) * 8
-                home = ratio[base : base + 8, :]
+                start_at = ((f - 12) * 8 + x) * 8
+                home = ratio[start_at : start_at + 8, :]
             wide[x, f, 0:8, :] = south
             wide[x, f, 8:16, :] = home
             wide[x, f, 16:24, :] = north
+    moves = fetch((wide,), (wide_hbm,), sems_out)
     even_x = lax.rem(lax.axis_index("gx"), 2) == 0
     for buffer, east in ((send_a, even_x), (send_b, jnp.logical_not(even_x))):
         first = jnp.where(east, 8 - EARLY, 0)
@@ -227,6 +378,36 @@
                 buffer[at + 8 : at + 16, :] = jnp.where(
                     row < 4, wide[first + d, 12 + c, 16:24, :], wide[first + d, 12 + c, 0:8, :]
                 )
+    for n, (source, target) in enumerate(((send_a, send_a_hbm), (send_b, send_b_hbm))):
+        moves.append(pltpu.make_async_copy(source, target, sems_out.at[1 + n]))
+        moves[-1].start()
+    gx = lax.axis_index("gx")
+    px_west = jnp.where(even_x, edge_b[...], edge_a[...]) * (gx > 0).astype(F32)
+    px_east = jnp.where(even_x, edge_a[...], edge_b[...]) * (gx < 7).astype(F32)
+    lane = lanes_of()
+    totals = []
+    for x in range(8):
+        east = px[x + 1] if x < 7 else px_east
+        west = px[x - 1] if x > 0 else px_west
+        value = px[x] * east + px[x] * west
+        along = tuple(wide[x, 10, 8 * t : 8 * t + 8, :] for t in range(3))
+        value = value + along[1] * north_of(along, row)[1] + along[1] * south_of(along, row)[1]
+        value = value + jnp.where(lane < 127, pz[x] * pltpu.roll(pz[x], 127, 1), 0.0)
+        value = value + jnp.where(lane > 0, pz[x] * pltpu.roll(pz[x], 1, 1), 0.0)
+        totals.append(value)
+    for pair in range(4):
+        total = jnp.concatenate(totals[pair * 2 : pair * 2 + 2], axis=0)
+        for c in range(NC):
+            here = slice((c * 4 + pair) * 16, (c * 4 + pair) * 16 + 16)
+            diagonal = accum[here, :].astype(F32) + mobil[here, :].astype(F32) * total
+            inverse = OMEGA / diagonal
+            scale[here, :] = inverse
+            base[here, :] = inverse * cot[here, :].astype(F32)
+    for n, (source, target) in enumerate(((scale, scale_hbm), (base, base_hbm))):
+        moves.append(pltpu.make_async_copy(source, target, sems_out.at[3 + n]))
+        moves[-1].start()
+    for move in moves:
+        move.wait()
 
 
 def north_of(tiles, row):
@@ -242,8 +423,10 @@
 
 
 def early_kernel(
-    wide, recv_a, recv_b, trans, gain, begin, begin_edge, iters, perms, ratios
+    wide_hbm, recv_a, recv_b, trans, gain, begin, begin_edge, iters, perms, ratios, wide, sem
 ):
+    copy = pltpu.make_async_copy(wide_hbm, wide, sem)
+    copy.start()
     row = rows_of()
     lane = lanes_of()
     gx = lax.axis_index("gx")
@@ -278,6 +461,7 @@
         return 0
 
     lax.fori_loop(0, LATE, bring_ratio, 0)
+    copy.wait()
 
     def settle(x, _):
         for f in range(NC):
@@ -364,24 +548,47 @@
 
 
 def scatter_kernel(
-    cell, arrived, wide, recv_a, recv_b, cot, accum, mobil, weight, send_a, send_b, left, right, total
+    cell,
+    arrived,
+    scale_hbm,
+    base_hbm,
+    weight,
+    send_a,
+    send_b,
+    left,
+    right,
+    scale,
+    base,
+    sems,
 ):
-    row = rows_of()
-    lane = lanes_of()
+    copies = fetch(
+        (scale_hbm, base_hbm),
+        (scale, base),
+        sems,
+    )
     row16 = rows_of((16, 128))
-    gx = lax.axis_index("gx")
-    even_x = lax.rem(gx, 2) == 0
-
+
+    def mark(j, _):
+        for half in range(2):
+            at = pl.ds(pl.multiple_of(j * 256 + half * 128, 128), 128)
+            place = jnp.broadcast_to(cell[j, half : half + 1, :], (16, 128))
+            high = lax.bitwise_or(
+                lax.bitwise_and(place, 127),
+                lax.shift_left(lax.shift_right_logical(place, 11), 7),
+            )
+            for n in range(32):
+                right[n * 16 : n * 16 + 16, at] = jnp.where(
+                    high == row16 + n * 16, 1.0, 0.0
+                ).astype(BF16)
+        return 0
+
+    lax.fori_loop(0, BRICKS, mark, 0)
     def build(j, _):
         for half in range(2):
             at = pl.ds(pl.multiple_of(j * 256 + half * 128, 128), 128)
             place = cell[j, half : half + 1, :]
             place = jnp.broadcast_to(place, (16, 128))
             low = lax.bitwise_and(lax.shift_right_logical(place, 7), 15)
-            high = lax.bitwise_or(
-                lax.bitwise_and(place, 127),
-                lax.shift_left(lax.shift_right_logical(place, 11), 7),
-            )
             mine = low == row16
             values = arrived[j, pl.ds(half, NC, stride=2), :]
             coarse = values.astype(BF16).astype(F32)
@@ -392,33 +599,14 @@
                     left[part * 144 + c * 16 : part * 144 + c * 16 + 16, at] = jnp.where(
                         mine, line, 0.0
                     ).astype(BF16)
-            for n in range(32):
-                right[n * 16 : n * 16 + 16, at] = jnp.where(
-                    high == row16 + n * 16, 1.0, 0.0
-                ).astype(BF16)
         return 0
 
     lax.fori_loop(0, BRICKS, build, 0)
 
-    west_in = (gx > 0).astype(F32)
-    east_in = (gx < 7).astype(F32)
-    at_west = slice(((EARLY - 1) * 12 + 9) * 24 + 8, ((EARLY - 1) * 12 + 9) * 24 + 16)
-    at_east = slice(9 * 24 + 8, 9 * 24 + 16)
-    px_west = jnp.where(even_x, recv_b[at_west, :], recv_a[at_west, :]) * west_in
-    px_east = jnp.where(even_x, recv_a[at_east, :], recv_b[at_east, :]) * east_in
-    for x in range(8):
-        px = wide[x, 9, 8:16, :]
-        east = wide[x + 1, 9, 8:16, :] if x < 7 else px_east
-        west = wide[x - 1, 9, 8:16, :] if x > 0 else px_west
-        value = px * east + px * west
-        py = tuple(wide[x, 10, 8 * t : 8 * t + 8, :] for t in range(3))
-        value = value + py[1] * north_of(py, row)[1] + py[1] * south_of(py, row)[1]
-        pz = wide[x, 11, 8:16, :]
-        value = value + jnp.where(lane < 127, pz * pltpu.roll(pz, 127, 1), 0.0)
-        value = value + jnp.where(lane > 0, pz * pltpu.roll(pz, 1, 1), 0.0)
-        total[x * 8 : x * 8 + 8, :] = value
-
     for part in range(2):
+        if part == 0:
+            copies[0].wait()
+            copies[1].wait()
         product = lax.dot_general(
             left[...],
             right[part * 256 : part * 256 + 256, :],
@@ -431,10 +619,7 @@
             for c in range(NC):
                 well = product[c * 16 : c * 16 + 16, at] + product[144 + c * 16 : 160 + c * 16, at]
                 here = slice((c * 4 + pair) * 16, (c * 4 + pair) * 16 + 16)
-                diagonal = accum[here, :].astype(F32) + mobil[here, :].astype(F32) * total[
-                    pair * 16 : pair * 16 + 16, :
-                ]
-                weight[here, :] = OMEGA * (cot[here, :].astype(F32) - well) / diagonal
+                weight[here, :] = base[here, :] - scale[here, :] * well
 
     even = lax.rem(lax.axis_index("gy"), 2) == 0
     for buffer in (send_a, send_b):
@@ -471,7 +656,7 @@
 
 
 def sweep_kernel(
-    trans, gain, begin, begin_edge, wide, edge, recv_a, recv_b, result, weight, one, two
+    trans, gain, begin, begin_edge, wide, edge, recv_a, recv_b, result, weight, one, two, last_one, sems
 ):
     row = rows_of()
     even = lax.rem(lax.axis_index("gx"), 2) == 0
@@ -523,13 +708,18 @@
                 part = slice(8 * t, 8 * t + 8)
                 value = KEEP * mid[t] + weight[at, c, part, :] + gain[at, c, part, :] * value
                 if final:
-                    result[c, at - LATE] = value
+                    last_one[at - LATE, c] = value
                 else:
                     new[at, c, part, :] = value
+
+    def writing(x):
+        return pltpu.make_async_copy(last_one.at[x], result.at[:, x], sems.at[x])
 
     def sweep(begin_at, end_at, held, new, brim=False, final=False):
         def body(at, _):
             column(at, held, new, brim, final)
+            if final:
+                writing(at - LATE).start()
             return 0
 
         lax.fori_loop(begin_at, end_at, body, 0)
@@ -541,6 +731,8 @@
     sweep(3, COLS - 3, one, two)
     sweep(4, COLS - 4, two, one)
     sweep(5, COLS - 5, one, None, final=True)
+    for x in range(8):
+        writing(x).wait()
 
 
 def swap_pairs(shards, axis):
@@ -570,49 +762,98 @@
     cot = cell_cot.reshape(NC * 64, 128)
     accum = accumulation.reshape(NC * 64, 128)
     mobil = mobility.reshape(NC * 64, 128)
-    ratio, early_a, early_b = call(
-        early_pack_kernel,
-        (out(NC * 64, 128), out(EARLY_ROWS, 128), out(EARLY_ROWS, 128)),
-        [],
-        [VMEM] * 6,
-        "early_pack",
-    )(start_iterate, perm_x, perm_y, perm_z, accum, mobil)
+    held = [
+        pltpu.VMEM((NC, 8, 8, 128), F32),
+        pltpu.VMEM((8, 8, 128), F32),
+        pltpu.VMEM((8, 8, 128), F32),
+        pltpu.VMEM((8, 8, 128), F32),
+        pltpu.VMEM((NC * 64, 128), BF16),
+        pltpu.VMEM((NC * 64, 128), BF16),
+    ]
+    given = [pin(x) for x in (start_iterate, perm_x, perm_y, perm_z, accum, mobil)]
+    mats, vecs, head, ratio, early_a, early_b, edge_a, edge_b = call(
+        first_kernel,
+        (
+            out(81, 8, 128),
+            out(NC, 8, 128),
+            out(BRICKS, 8, 128),
+            out(NC * 64, 128),
+            out(EARLY_ROWS, 128),
+            out(EARLY_ROWS, 128),
+            out(8, 128),
+            out(8, 128),
+        ),
+        [
+            pltpu.VMEM((90, 8, 128), F32),
+            pltpu.SMEM((8,), I32),
+            pltpu.VMEM((NC, 8, 128), F32),
+            pltpu.VMEM((NC, NC, 8, 128), F32),
+            pltpu.VMEM((NC, NC, 8, 128), F32),
+        ]
+        + held
+        + [pltpu.SemaphoreType.DMA((10,))],
+        [HBM] * 10,
+        "first",
+        10_000_000,
+    )(pin(well_len), pin(seg_source), pin(seg_inverse), pin(seg_outflow), *given)
+    heads = lax.all_to_all(head, "gy", 0, 0, tiled=True)
     early_a, early_b = swap_pairs((early_a, early_b), "gy")
-
-    mats, vecs, head = call(
-        scan_kernel,
-        (out(81, 8, 128), out(NC, 8, 128), out(BRICKS, 8, 128)),
-        [pltpu.VMEM((90, 8, 128), F32)],
-        [SMEM, VMEM, VMEM, VMEM],
-        "well_scan",
-        10_000_000,
-    )(well_len, seg_source, seg_inverse, seg_outflow)
-    heads = lax.all_to_all(head, "gy", 0, 0, tiled=True)
-
-    wide, wide_a, wide_b = call(
-        early_wide_kernel,
-        (out(8, FIELDS, 24, 128), out(WIDE_ROWS, 128), out(WIDE_ROWS, 128)),
-        [],
-        [VMEM] * 7,
-        "early_wide",
-    )(start_iterate, perm_x, perm_y, perm_z, ratio, early_a, early_b)
-    wide_a, wide_b = swap_pairs((wide_a, wide_b), "gx")
-
-    lam, sent = call(
+    edge_a, edge_b = swap_pairs((edge_a, edge_b), "gx")
+
+    lam, sent, token = call(
         rows_kernel,
-        (out(NC, 8, 128), out(BRICKS * SLOT, 128)),
-        [],
-        [SMEM] + [VMEM] * 5,
+        (far(NC, 8, 128), far(BRICKS * SLOT, 128), out(8, 128)),
+        [
+            pltpu.VMEM((NC, 8, 128), F32),
+            pltpu.VMEM((BRICKS * SLOT, 128), F32),
+            pltpu.SMEM((BRICKS,), I32),
+            pltpu.VMEM((BRICKS, 256), I32),
+            pltpu.SemaphoreType.DMA,
+            pltpu.SemaphoreType.DMA((2,)),
+            pltpu.SemaphoreType.DMA((2,)),
+        ],
+        [HBM, HBM] + [VMEM] * 6,
         "well_rows",
+        out_specs=(HBM, HBM, VMEM),
     )(
-        perf_count.reshape(BRICKS),
+        pin(perf_count.reshape(BRICKS)),
+        pin(perf_seg.reshape(BRICKS, 256)),
         mats,
         vecs,
         heads,
-        perf_seg.reshape(BRICKS, 256),
         perf_coupling.reshape(NC, NC, BRICKS, 256),
+        edge_a,
+        edge_b,
     )
     arrived = lax.all_to_all(sent, "gy", 0, 0, tiled=True)
+
+    cell = recv_cell.reshape(BRICKS, 2, 128)
+    wide, wide_a, wide_b, scale, base = call(
+        shade_kernel,
+        (
+            far(8, FIELDS, 24, 128),
+            far(WIDE_ROWS, 128),
+            far(WIDE_ROWS, 128),
+            far(NC * 64, 128),
+            far(NC * 64, 128),
+        ),
+        held
+        + [
+            pltpu.VMEM((NC * 64, 128), BF16),
+            pltpu.VMEM((8, FIELDS, 24, 128), F32),
+            pltpu.VMEM((WIDE_ROWS, 128), F32),
+            pltpu.VMEM((WIDE_ROWS, 128), F32),
+            pltpu.VMEM((NC * 64, 128), F32),
+            pltpu.VMEM((NC * 64, 128), F32),
+            pltpu.SemaphoreType.DMA((7,)),
+            pltpu.SemaphoreType.DMA((5,)),
+        ],
+        [VMEM] + [HBM] * 7 + [VMEM] * 5,
+        "shade",
+        limit=12,
+        out_specs=(HBM,) * 5,
+    )(token, *given, pin(cot), ratio, early_a, early_b, edge_a, edge_b)
+    wide_a, wide_b = swap_pairs((wide_a, wide_b), "gx")
 
     weight, late_a, late_b = call(
         scatter_kernel,
@@ -620,12 +861,15 @@
         [
             pltpu.VMEM((288, 4096), BF16),
             pltpu.VMEM((512, 4096), BF16),
-            pltpu.VMEM((64, 128), F32),
+            pltpu.VMEM((NC * 64, 128), F32),
+            pltpu.VMEM((NC * 64, 128), F32),
+            pltpu.SemaphoreType.DMA((2,)),
         ],
-        [VMEM] * 8,
+        [VMEM] * 2 + [HBM] * 2,
         "scatter",
-        limit=32,
-    )(recv_cell.reshape(BRICKS, 2, 128), arrived.reshape(BRICKS, SLOT, 128), wide, wide_a, wide_b, cot, accum, mobil)
+        20_000_000_000,
+        limit=16,
+    )(cell, arrived.reshape(BRICKS, SLOT, 128), pin(scale), pin(base))
     late_a, late_b = swap_pairs((late_a, late_b), "gy")
 
     trans, gain, begin, begin_edge = call(
@@ -640,11 +884,13 @@
             pltpu.VMEM((8 + 2 * EARLY, NC, 24, 128), F32),
             pltpu.VMEM((8 + 2 * EARLY, 3, 24, 128), F32),
             pltpu.VMEM((2 * LATE, NC, 16, 128), F32),
+            pltpu.VMEM((8, FIELDS, 24, 128), F32),
+            pltpu.SemaphoreType.DMA,
         ],
-        [VMEM] * 3,
+        [HBM, VMEM, VMEM],
         "early",
-        limit=24,
-    )(wide, wide_a, wide_b)
+        limit=10,
+    )(pin(wide), wide_a, wide_b)
 
     widened, edge, side_a, side_b = call(
         late_wide_kernel,
@@ -664,10 +910,11 @@
     result = call(
         sweep_kernel,
         out(NC, 8, 8, 128),
-        [wide_field] * 3,
+        [wide_field] * 3
+        + [pltpu.VMEM((8, NC, 8, 128), F32), pltpu.SemaphoreType.DMA((8,))],
         [VMEM] * 8,
         "sweeps",
-        limit=24,
+        out_specs=HBM,
     )(trans, gain, begin, begin_edge, widened, edge, side_a, side_b)
     return lam, result
 

time: 99 us -> 74.2 us (0.75)
  waiting for transfers between devices: 31.4 us -> 12.5 us
  starting transfers between devices: 16.7 us -> 30.8 us
  blocking collectives: 13.4 us -> 0 us
  local copies, waits for them, and re-layouts: 8.51 us -> 0.02 us
  Pallas kernels: 27.1 us -> 29.4 us
    all_to_all x1 -> x0, blocking collectives: 13.4 us -> none  [body(): heads = lax.all_to_all(head, 'gy', 0, 0, tiled=True)]
    ppermute x4 -> x5, waiting for transfers between devices: 10.8 us -> 0.01 us  [swap_pairs(): lax.ppermute(shards[0], axis, inner)]
    ppermute x4 -> x5, starting transfers between devices: 10.8 us -> 20.2 us  [swap_pairs(): lax.ppermute(shards[1], axis, outer)]
    unnamed x36 -> x4, local copies, waits for them, and re-layouts: 8.5 us -> 0.01 us
    all_to_all x1, waiting for transfers between devices: 8.27 us -> 0.21 us  [body(): arrived = lax.all_to_all(sent, 'gy', 0, 0, tiled=True)]
    ppermute x4 -> x5, waiting for transfers between devices: 12.3 us -> 7.04 us  [swap_pairs(): lax.ppermute(shards[1], axis, outer)]
    all_to_all x0 -> x1, waiting for transfers between devices: none -> 5.24 us  [body(): heads = lax.all_to_all(head, 'gy', 0, 0, tiled=True)]
    all_to_all x0 -> x1, starting transfers between devices: none -> 3.5 us  [body(): heads = lax.all_to_all(head, 'gy', 0, 0, tiled=True)]
  transfers between devices with their start and end apart: 9 -> 12, of which waited for: 6 -> 5; matrix products, arithmetic and copies ran while one was open for 0% -> 0% of each run, Pallas kernels for 13% -> 22%
where the time goes in v1:
time: 74.2 us; the launch traced here: 73.6 us
  starting transfers between devices  30.8 us (42%)
  Pallas kernels  29.4 us (40%)
  waiting for transfers between devices  12.5 us (17%)
  between operations  0.77 us (1%)
    ppermute x5, starting transfers between devices, swap_pairs(): lax.ppermute(shards[1], axis, outer)  20.2 us
    pallas_call x1, Pallas kernels, body(): call(sweep_kernel, out(NC, 8, 8, 128), [wide_field] * 3 + [pltpu.VMEM((8,...  7.46 us
    ppermute x5, waiting for transfers between devices, swap_pairs(): lax.ppermute(shards[1], axis, outer)  7.04 us
    pallas_call x1, Pallas kernels, body(): call(first_kernel, (out(81, 8, 128), out(NC, 8, 128), out(BRICKS, 8, 128)...  5.69 us
    all_to_all x1, waiting for transfers between devices, body(): heads = lax.all_to_all(head, 'gy', 0, 0, tiled=True)  5.24 us
    pallas_call x1, Pallas kernels, body(): call(rows_kernel, (far(NC, 8, 128), far(BRICKS * SLOT, 128), out(8, 128))...  4.49 us
    pallas_call x1, Pallas kernels, body(): call(early_kernel, (out(COLS, 6, 16, 128), out(COLS, NC, 16, 128), out(CO...  4.13 us
    pallas_call x1, Pallas kernels, body(): call(shade_kernel, (far(8, FIELDS, 24, 128), far(WIDE_ROWS, 128), far(WID...  3.8 us
  transfers between devices with their start and end apart: 12, of which 5 were waited for; matrix products, arithmetic and copies ran while one was open for 0% of the time, Pallas kernels for 22%

profile of v1, /device:TPU:0, one launch (start us, length us, event | category | flops | bytes accessed | tf_op | source)
XLA Modules:
  0.0 73.6 jit_solution(12822948021299353778)
XLA Ops:
  0.6 5.7 %first.1 = (f32[81,8,128]{2,1,0:T(8,128)S(1)}, f32[9,8,128]{2,1,0:T(8,128)S(1)}, f32[16,8,128]{2,1,0:T(8,128)}, f32[576,128]{1,0:T(8,128)S(1)}, f32[1024,128]{1,...) custom-call(s32[8]{0:T(128)} %len_hbm.1, f32[9,8,128]{2,1,0:T(8,128)} %src_hbm.1, ...), custom_call_target="tpu_custom_call" | custom-call | flops 10000000 | bytes 1000000 | tf_op jit(solution)/shard_map/first/pallas_call | solution.py:774
  6.3 0.0 copy-start.1
  6.4 1.7 %collective-permute-start.2 = (f32[1024,128]{1,0:T(8,128)}, f32[1024,128]{1,0:T(8,128)S(1)}, u32[]{:S(2)}, u32[]{:S(2)}) collective-permute-start(f32[1024,128]{1,0:T(8,128)} %get-tuple-element.37), channel_id=1, source_target_pairs={{0,1},{1,0},{2,3},{3,2},{4,5},{5,4},{6,7},{7,6},{8,9},{9,8},{10,11... | collective-permute-start | bytes 1572872 | tf_op jit(solution)/shard_map/ppermute | solution.py:742
  8.0 4.5 %collective-permute-start.3 = (f32[1024,128]{1,0:T(8,128)}, f32[1024,128]{1,0:T(8,128)S(1)}, u32[]{:S(2)}, u32[]{:S(2)}) collective-permute-start(f32[1024,128]{1,0:T(8,128)} %get-tuple-element.38), channel_id=1, source_target_pairs={{0,15},{1,2},{2,1},{3,4},{4,3},{5,6},{6,5},{7,8},{8,7},{9,10},{10,... | collective-permute-start | bytes 1572872 | tf_op jit(solution)/shard_map/ppermute | solution.py:742
  12.6 3.5 %all-to-all-start = ((f32[16,8,128]{2,1,0:T(8,128)}), f32[16,8,128]{2,1,0:T(8,128)S(1)}, u32[]{:S(2)}, u32[]{:S(2)}) async-start(f32[16,8,128]{2,1,0:T(8,128)} %get-tuple-element.31), calls=%async_computation | async-start | bytes 131072 | tf_op jit(solution)/shard_map/all_to_all | solution.py:799
  16.1 0.1 collective-permute-start
  16.2 4.1 %collective-permute-start.1 = (f32[8,128]{1,0:T(8,128)S(1)}, f32[8,128]{1,0:T(8,128)S(1)}, u32[]{:S(2)}, u32[]{:S(2)}) collective-permute-start(f32[8,128]{1,0:T(8,128)S(1)} %get-tuple-element.33), channel_id=1, source_target_pairs={{0,112},{16,32},{32,16},{48,64},{64,48},{80,96},{96,80},{112,0},{1... | collective-permute-start | bytes 12296 | tf_op jit(solution)/shard_map/ppermute | solution.py:742
  20.3 0.0 collective-permute-done.edge_a
  20.3 1.3 %collective-permute-done.1.edge_b = f32[8,128]{1,0:T(8,128)S(1)} collective-permute-done((f32[8,128]{1,0:T(8,128)S(1)}, f32[8,128]{1,0:T(8,128)S(1)}, u32[]{:S(2)}, u32[]{:S(2)}) %collective-permute-start.1) | collective-permute-done | bytes 4128 | tf_op jit(solution)/shard_map/ppermute | solution.py:742
  21.6 5.2 %all-to-all-done.heads = f32[16,8,128]{2,1,0:T(8,128)S(1)} async-done(((f32[16,8,128]{2,1,0:T(8,128)}), f32[16,8,128]{2,1,0:T(8,128)S(1)}, u32[]{:S(2)}, u32[]{:S(2)}) %all-to-all-start) | async-done | bytes 65568 | tf_op jit(solution)/shard_map/all_to_all | solution.py:799
  26.9 4.5 %well_rows.1 = (f32[9,8,128]{2,1,0:T(8,128)}, f32[384,128]{1,0:T(8,128)}, f32[8,128]{1,0:T(8,128)S(1)}) custom-call(s32[16]{0:T(128)} %bitcast.17, s32[16,256]{1,0:T(8,128)} %bitcast.16, f32[81,8,128]{2,1,0:T(8,128)S(1)} %get-tuple-element.29.mats, f32[9,8,128]{2,1,0:T(8,128)S(1)} %get-tuple-element.30.vecs, f32[16,8,128]{2,1,0:T(8,128)S(1)} %all-to-all-done.heads, ...), custom_call_target="tpu_custom_call" | custom-call | flops 1000000 | bytes 1000000 | tf_op jit(solution)/shard_map/well_rows/pallas_call | solution.py:803
  31.4 3.5 %all-to-all-start.1 = ((f32[16,24,128]{2,1,0:T(8,128)}), f32[16,24,128]{2,1,0:T(8,128)S(1)}, u32[]{:S(2)}, u32[]{:S(2)}) async-start(f32[16,24,128]{2,1,0:T(8,128)} %bitcast.14), calls=%async_computation.1 | async-start | bytes 393216 | tf_op jit(solution)/shard_map/all_to_all | solution.py:828
  34.9 0.0 collective-permute-done.2.recv_a
  34.9 0.0 collective-permute-done.3.recv_b
  35.0 3.8 %shade.1 = (f32[8,21,24,128]{3,2,1,0:T(8,128)}, f32[2448,128]{1,0:T(8,128)}, f32[2448,128]{1,0:T(8,128)}, f32[576,128]{1,0:T(8,128)}, f32[576,128]{1,0:T(8,128)}) custom-call(f32[8,128]{1,0:T(8,128)S(1)} %get-tuple-element.35.after, f32[9,8,8,128]{3,2,1,0:T(8,128)} %start_hbm.3, f32[8,8,128]{2,1,0:T(8,128)} %px_hbm.3, f32[8,8,128]{2,1,0:T(8,128)} %py_hbm.3, ...), custom_call_target="tpu_custom_call" | custom-call | flops 1000000 | bytes 1000000 | tf_op jit(solution)/shard_map/shade/pallas_call | solution.py:831
  38.8 0.1 collective-permute-start.4
  38.9 4.1 %collective-permute-start.5 = (f32[2448,128]{1,0:T(8,128)}, f32[2448,128]{1,0:T(8,128)S(1)}, u32[]{:S(2)}, u32[]{:S(2)}) collective-permute-start(f32[2448,128]{1,0:T(8,128)} %get-tuple-element.41), channel_id=1, source_target_pairs={{0,112},{16,32},{32,16},{48,64},{64,48},{80,96},{96,80},{112,0},{1... | collective-permute-start | bytes 3760136 | tf_op jit(solution)/shard_map/ppermute | solution.py:742
  43.0 0.2 all-to-all-done.1.arrived
  43.2 3.7 %scatter.1 = (f32[576,128]{1,0:T(8,128)S(1)}, f32[376,128]{1,0:T(8,128)S(1)}, f32[376,128]{1,0:T(8,128)S(1)}) custom-call(s32[16,2,128]{2,1,0:T(2,128)S(1)} %reshape.35.cell, f32[16,24,128]{2,1,0:T(8,128)S(1)} %all-to-all-done.1.arrived, f32[576,128]{1,0:T(8,128)} %get-tuple-element.47.scale_hbm, f32[576,128]{1,0:T(8,128)} %get-tuple-element.48.base_hbm), custom_call_target="tpu_custom_call" | custom-call | flops 20000000000 | bytes 1000000 | tf_op jit(solution)/shard_map/scatter/pallas_call | solution.py:858
  46.9 1.7 %collective-permute-start.6 = (f32[376,128]{1,0:T(8,128)S(1)}, f32[376,128]{1,0:T(8,128)S(1)}, u32[]{:S(2)}, u32[]{:S(2)}) collective-permute-start(f32[376,128]{1,0:T(8,128)S(1)} %get-tuple-element.50), channel_id=1, source_target_pairs={{0,1},{1,0},{2,3},{3,2},{4,5},{5,4},{6,7},{7,6},{8,9},{9,8},{10,11... | collective-permute-start | bytes 577544 | tf_op jit(solution)/shard_map/ppermute | solution.py:742
  48.6 4.3 %collective-permute-start.7 = (f32[376,128]{1,0:T(8,128)S(1)}, f32[376,128]{1,0:T(8,128)S(1)}, u32[]{:S(2)}, u32[]{:S(2)}) collective-permute-start(f32[376,128]{1,0:T(8,128)S(1)} %get-tuple-element.51), channel_id=1, source_target_pairs={{0,15},{1,2},{2,1},{3,4},{4,3},{5,6},{6,5},{7,8},{8,7},{9,10},{10,... | collective-permute-start | bytes 577544 | tf_op jit(solution)/shard_map/ppermute | solution.py:742
  52.8 0.0 collective-permute-done.6.recv_a
  52.8 4.7 %collective-permute-done.7.recv_b = f32[376,128]{1,0:T(8,128)S(1)} collective-permute-done((f32[376,128]{1,0:T(8,128)S(1)}, f32[376,128]{1,0:T(8,128)S(1)}, u32[]{:S(2)}, u32[]{:S(2)}) %collective-permute-start.7) | collective-permute-done | bytes 192544 | tf_op jit(solution)/shard_map/ppermute | solution.py:742
  57.5 0.2 late_wide.1
  57.7 0.1 collective-permute-start.8
  57.8 3.1 %collective-permute-start.9 = (f32[5,9,16,128]{3,2,1,0:T(8,128)S(1)}, f32[5,9,16,128]{3,2,1,0:T(8,128)S(1)}, u32[]{:S(2)}, u32[]{:S(2)}) collective-permute-start(f32[5,9,16,128]{3,2,1,0:T(8,128)S(1)} %get-tuple-element.55), channel_id=1, source_target_pairs={{0,112},{16,32},{32,16},{48,64},{64,48},{80,96},{96,80},{112,0},{1... | collective-permute-start | bytes 1105928 | tf_op jit(solution)/shard_map/ppermute | solution.py:742
  60.9 0.0 collective-permute-done.4.recv_a
  60.9 0.0 collective-permute-done.5.recv_b
  60.9 4.1 %early.1 = (f32[18,6,16,128]{3,2,1,0:T(8,128)S(1)}, f32[18,9,16,128]{3,2,1,0:T(8,128)S(1)}, f32[18,9,16,128]{3,2,1,0:T(8,128)S(1)}, f32[8,9,8,128]{3,2,1,0:T(8,128)S(1)}) custom-call(f32[8,21,24,128]{3,2,1,0:T(8,128)} %get-tuple-element.39.wide_hbm, f32[2448,128]{1,0:T(8,128)S(1)} %collective-permute-done.4.recv_a, f32[2448,128]{1,0:T(8,128)S(1)} %collective-permute-done.5.recv_b), custom_call_target="tpu_custom_call" | custom-call | flops 1000000 | bytes 1000000 | tf_op jit(solution)/shard_map/early/pallas_call | solution.py:875
  65.1 0.0 collective-permute-done.8.recv_a
  65.1 1.0 %collective-permute-done.9.recv_b = f32[5,9,16,128]{3,2,1,0:T(8,128)S(1)} collective-permute-done((f32[5,9,16,128]{3,2,1,0:T(8,128)S(1)}, f32[5,9,16,128]{3,2,1,0:T(8,128)S(1)}, u32[]{:S(2)}, u32[]{:S(2)}) %collective-permute-start.9) | collective-permute-done | bytes 368672 | tf_op jit(solution)/shard_map/ppermute | solution.py:742
  66.1 7.5 %sweeps.1 = f32[9,8,8,128]{3,2,1,0:T(8,128)} custom-call(f32[18,6,16,128]{3,2,1,0:T(8,128)S(1)} %get-tuple-element.42.trans, f32[18,9,16,128]{3,2,1,0:T(8,128)S(1)} %get-tuple-element.43.gain, f32[18,9,16,128]{3,2,1,0:T(8,128)S(1)} %get-tuple-element.44.begin, f32[8,9,8,128]{3,2,1,0:T(8,128)S(1)} %get-tuple-element.45.begin_edge, ...), custom_call_target="tpu_custom_call" | custom-call | flops 1000000 | bytes 1000000 | tf_op jit(solution)/shard_map/sweeps/pallas_call | solution.py:910
  (4 shorter events, 0.0 us)
Async XLA Ops:
  0.6 26.2 %copy-start = (f32[9,9,1,1,16,256]{5,4,3,2,1,0:T(8,128)S(1)}, f32[9,9,1,1,16,256]{5,4,3,2,1,0:T(8,128)}, u32[]{:S(2)}) copy-start(f32[9,9,1,1,16,256]{5,4,3,2,1,0:T(8,128)} %param.21) | copy-start | bytes 3981316
  6.3 28.6 %copy-start.1 = (s32[1,1,16,256]{3,2,1,0:T(8,128)S(1)}, s32[1,1,16,256]{3,2,1,0:T(8,128)}, u32[]{:S(2)}) copy-start(s32[1,1,16,256]{3,2,1,0:T(8,128)} %param.22) | copy-start | bytes 49156
  6.4 28.6 %collective-permute-start.2 = (f32[1024,128]{1,0:T(8,128)}, f32[1024,128]{1,0:T(8,128)S(1)}, u32[]{:S(2)}, u32[]{:S(2)}) collective-permute-start(f32[1024,128]{1,0:T(8,128)} %get-tuple-element.37), channel_id=1, source_target_pairs={{0,1},{1,0},{2,3},{3,2},{4,5},{5,4},{6,7},{7,6},{8,9},{9,8},{10,11... | collective-permute-start | bytes 1572872 | tf_op jit(solution)/shard_map/ppermute | solution.py:742
  8.0 26.9 %collective-permute-start.3 = (f32[1024,128]{1,0:T(8,128)}, f32[1024,128]{1,0:T(8,128)S(1)}, u32[]{:S(2)}, u32[]{:S(2)}) collective-permute-start(f32[1024,128]{1,0:T(8,128)} %get-tuple-element.38), channel_id=1, source_target_pairs={{0,15},{1,2},{2,1},{3,4},{4,3},{5,6},{6,5},{7,8},{8,7},{9,10},{10,... | collective-permute-start | bytes 1572872 | tf_op jit(solution)/shard_map/ppermute | solution.py:742
  12.6 14.3 %all-to-all-start = ((f32[16,8,128]{2,1,0:T(8,128)}), f32[16,8,128]{2,1,0:T(8,128)S(1)}, u32[]{:S(2)}, u32[]{:S(2)}) async-start(f32[16,8,128]{2,1,0:T(8,128)} %get-tuple-element.31), calls=%async_computation | async-start | bytes 131072 | tf_op jit(solution)/shard_map/all_to_all | solution.py:799
  16.1 4.2 %collective-permute-start = (f32[8,128]{1,0:T(8,128)S(1)}, f32[8,128]{1,0:T(8,128)S(1)}, u32[]{:S(2)}, u32[]{:S(2)}) collective-permute-start(f32[8,128]{1,0:T(8,128)S(1)} %get-tuple-element.32), channel_id=1, source_target_pairs={{0,16},{16,0},{32,48},{48,32},{64,80},{80,64},{96,112},{112,96},{1... | collective-permute-start | bytes 12296 | tf_op jit(solution)/shard_map/ppermute | solution.py:742
  16.2 5.5 %collective-permute-start.1 = (f32[8,128]{1,0:T(8,128)S(1)}, f32[8,128]{1,0:T(8,128)S(1)}, u32[]{:S(2)}, u32[]{:S(2)}) collective-permute-start(f32[8,128]{1,0:T(8,128)S(1)} %get-tuple-element.33), channel_id=1, source_target_pairs={{0,112},{16,32},{32,16},{48,64},{64,48},{80,96},{96,80},{112,0},{1... | collective-permute-start | bytes 12296 | tf_op jit(solution)/shard_map/ppermute | solution.py:742
  31.4 11.8 %all-to-all-start.1 = ((f32[16,24,128]{2,1,0:T(8,128)}), f32[16,24,128]{2,1,0:T(8,128)S(1)}, u32[]{:S(2)}, u32[]{:S(2)}) async-start(f32[16,24,128]{2,1,0:T(8,128)} %bitcast.14), calls=%async_computation.1 | async-start | bytes 393216 | tf_op jit(solution)/shard_map/all_to_all | solution.py:828
  38.8 22.1 %collective-permute-start.4 = (f32[2448,128]{1,0:T(8,128)}, f32[2448,128]{1,0:T(8,128)S(1)}, u32[]{:S(2)}, u32[]{:S(2)}) collective-permute-start(f32[2448,128]{1,0:T(8,128)} %get-tuple-element.40), channel_id=1, source_target_pairs={{0,16},{16,0},{32,48},{48,32},{64,80},{80,64},{96,112},{112,96},{1... | collective-permute-start | bytes 3760136 | tf_op jit(solution)/shard_map/ppermute | solution.py:742
  38.9 22.1 %collective-permute-start.5 = (f32[2448,128]{1,0:T(8,128)}, f32[2448,128]{1,0:T(8,128)S(1)}, u32[]{:S(2)}, u32[]{:S(2)}) collective-permute-start(f32[2448,128]{1,0:T(8,128)} %get-tuple-element.41), channel_id=1, source_target_pairs={{0,112},{16,32},{32,16},{48,64},{64,48},{80,96},{96,80},{112,0},{1... | collective-permute-start | bytes 3760136 | tf_op jit(solution)/shard_map/ppermute | solution.py:742
  46.9 5.9 %collective-permute-start.6 = (f32[376,128]{1,0:T(8,128)S(1)}, f32[376,128]{1,0:T(8,128)S(1)}, u32[]{:S(2)}, u32[]{:S(2)}) collective-permute-start(f32[376,128]{1,0:T(8,128)S(1)} %get-tuple-element.50), channel_id=1, source_target_pairs={{0,1},{1,0},{2,3},{3,2},{4,5},{5,4},{6,7},{7,6},{8,9},{9,8},{10,11... | collective-permute-start | bytes 577544 | tf_op jit(solution)/shard_map/ppermute | solution.py:742
  48.6 8.9 %collective-permute-start.7 = (f32[376,128]{1,0:T(8,128)S(1)}, f32[376,128]{1,0:T(8,128)S(1)}, u32[]{:S(2)}, u32[]{:S(2)}) collective-permute-start(f32[376,128]{1,0:T(8,128)S(1)} %get-tuple-element.51), channel_id=1, source_target_pairs={{0,15},{1,2},{2,1},{3,4},{4,3},{5,6},{6,5},{7,8},{8,7},{9,10},{10,... | collective-permute-start | bytes 577544 | tf_op jit(solution)/shard_map/ppermute | solution.py:742
  57.7 7.4 %collective-permute-start.8 = (f32[5,9,16,128]{3,2,1,0:T(8,128)S(1)}, f32[5,9,16,128]{3,2,1,0:T(8,128)S(1)}, u32[]{:S(2)}, u32[]{:S(2)}) collective-permute-start(f32[5,9,16,128]{3,2,1,0:T(8,128)S(1)} %get-tuple-element.54), channel_id=1, source_target_pairs={{0,16},{16,0},{32,48},{48,32},{64,80},{80,64},{96,112},{112,96},{1... | collective-permute-start | bytes 1105928 | tf_op jit(solution)/shard_map/ppermute | solution.py:742
  57.8 8.3 %collective-permute-start.9 = (f32[5,9,16,128]{3,2,1,0:T(8,128)S(1)}, f32[5,9,16,128]{3,2,1,0:T(8,128)S(1)}, u32[]{:S(2)}, u32[]{:S(2)}) collective-permute-start(f32[5,9,16,128]{3,2,1,0:T(8,128)S(1)} %get-tuple-element.55), channel_id=1, source_target_pairs={{0,112},{16,32},{32,16},{48,64},{64,48},{80,96},{96,80},{112,0},{1... | collective-permute-start | bytes 1105928 | tf_op jit(solution)/shard_map/ppermute | solution.py:742

commit v2 on v1

--- a/solution.py
+++ b/solution.py
@@ -18,8 +18,10 @@
 FIELDS = 21
 EARLY_ROWS = 16 + FIELDS * 8 * EARLY
 LATE_ROWS = 16 + NC * 8 * LATE
-RATIO_AT = 12 * EARLY * 24
-WIDE_ROWS = RATIO_AT + NC * LATE * 16
+SIDE_RATIO = 12 * EARLY * 8
+SIDE_ROWS = SIDE_RATIO + NC * LATE * 8
+CORNER_RATIO = 12 * EARLY * 16
+CORNER_ROWS = CORNER_RATIO + NC * LATE * 8
 COLS = 8 + 2 * LATE
 SLOT = 24
 
@@ -86,13 +88,18 @@
     mobil_hbm,
     mats,
     vecs,
+    head_hbm,
+    ratio,
+    send_a_hbm,
+    send_b_hbm,
+    side_a_hbm,
+    side_b_hbm,
+    rolled,
     head,
-    ratio,
     send_a,
     send_b,
-    edge_a,
-    edge_b,
-    rolled,
+    side_a,
+    side_b,
     len_ref,
     src,
     inv,
@@ -104,6 +111,7 @@
     accum,
     mobil,
     sems,
+    sems_out,
 ):
     copies = fetch(
         (
@@ -121,12 +129,21 @@
         (inv, outf, src, len_ref, start, px, py, pz, accum, mobil),
         sems,
     )
+    for copy in copies[4:]:
+        copy.wait()
+    early_pack(start, px, py, pz, accum, mobil, ratio, send_a, send_b, side_a, side_b)
+    moves = fetch(
+        (send_a, send_b, side_a, side_b),
+        (send_a_hbm, send_b_hbm, side_a_hbm, side_b_hbm),
+        sems_out,
+    )
     for copy in copies[:4]:
         copy.wait()
     scan_wells(len_ref, src, inv, outf, mats, vecs, head, rolled)
-    for copy in copies[4:]:
-        copy.wait()
-    early_pack(start, px, py, pz, accum, mobil, ratio, send_a, send_b, edge_a, edge_b)
+    moves.append(pltpu.make_async_copy(head, head_hbm, sems_out.at[4]))
+    moves[-1].start()
+    for move in moves:
+        move.wait()
 
 
 def scan_wells(len_ref, src, inv, outf, mats, vecs, head, rolled):
@@ -150,7 +167,12 @@
             mats[c * NC + k] = -active * total
         return 0
 
-    lax.fori_loop(0, NC, start, 0)
+    def starts(group, _):
+        for a in range(3):
+            start(group * 3 + a, 0)
+        return 0
+
+    lax.fori_loop(0, 3, starts, 0)
 
     def step(i, _):
         gap = lax.shift_left(jnp.int32(1), i)
@@ -175,7 +197,9 @@
                         vecs[group * 3 + a] = vecs[group * 3 + a] + total
             return 0
 
-        return lax.fori_loop(0, 3, rows, 0)
+        for group in range(3):
+            rows(group, 0)
+        return 0
 
     lax.fori_loop(0, 7, step, 0)
     packed = jnp.zeros(TILE, F32)
@@ -191,12 +215,10 @@
 def rows_kernel(
     count_hbm,
     seg_hbm,
+    coupling_hbm,
     mats,
     vecs,
     heads,
-    coupling,
-    edge_a,
-    edge_b,
     lam_hbm,
     sent_hbm,
     token,
@@ -204,17 +226,21 @@
     sent,
     count_ref,
     perf_seg,
+    coupling,
     sem,
     sems,
     sems_out,
 ):
-    copies = fetch((count_hbm, seg_hbm), (count_ref, perf_seg), sems)
+    copies = fetch(
+        (count_hbm, seg_hbm, coupling_hbm), (count_ref, perf_seg, coupling), sems
+    )
     row = rows_of()
     lane = lanes_of()
     me = lax.axis_index("gy")
 
-    def hop(t, incoming):
-        head = heads[BRICKS - 1 - t]
+    def hop(j, incoming):
+        head = heads[j]
+        later = j > me
         after = []
         for c in range(NC):
             total = jnp.broadcast_to(head[:, 81 + c : 82 + c], TILE)
@@ -222,10 +248,15 @@
                 at = c * NC + k
                 total = total + jnp.broadcast_to(head[:, at : at + 1], TILE) * incoming[k]
             after.append(total)
-        return tuple(after)
-
-    nothing = tuple(jnp.zeros(TILE, F32) for _ in range(NC))
-    incoming = lax.fori_loop(0, BRICKS - 1 - me, hop, nothing)
+        return tuple(jnp.where(later, new, old) for new, old in zip(after, incoming))
+
+    def hops(t, incoming):
+        for step in range(5):
+            incoming = hop(BRICKS - 1 - t * 5 - step, incoming)
+        return incoming
+
+    incoming = tuple(jnp.zeros(TILE, F32) for _ in range(NC))
+    incoming = lax.fori_loop(0, 3, hops, incoming)
     for c in range(NC):
         total = vecs[c]
         for k in range(NC):
@@ -234,8 +265,8 @@
     moves = [pltpu.make_async_copy(lam, lam_hbm, sem)]
     moves[0].start()
     token[...] = jnp.zeros(TILE, F32)
-    for copy in copies:
-        copy.wait()
+    copies[0].wait()
+    copies[1].wait()
     for block in range(2):
         count = jnp.zeros(TILE, I32)
         for b in range(8):
@@ -255,6 +286,8 @@
                     total = jnp.where(is_well[w], got, total)
                 picked.append(total)
             live = lane + half * 128 < count
+            if block == 0 and half == 0:
+                copies[2].wait()
             for c in range(NC):
                 total = coupling[(0, c) + at] * picked[0]
                 for k in range(1, NC):
@@ -270,10 +303,7 @@
         move.wait()
 
 
-def early_pack(start, px, py, pz, accum, mobil, ratio, send_a, send_b, edge_a, edge_b):
-    even_x = lax.rem(lax.axis_index("gx"), 2) == 0
-    edge_a[...] = jnp.where(even_x, px[7], px[0])
-    edge_b[...] = jnp.where(even_x, px[0], px[7])
+def early_pack(start, px, py, pz, accum, mobil, ratio, send_a, send_b, side_a, side_b):
     even = lax.rem(lax.axis_index("gy"), 2) == 0
     for i in range(NC * 4):
         at = slice(i * 16, i * 16 + 16)
@@ -294,6 +324,20 @@
             at = 8 + (f * 8 + x) * EARLY
             send_a[at : at + EARLY, :] = jnp.where(even, high, low)
             send_b[at : at + EARLY, :] = jnp.where(even, low, high)
+    even_x = lax.rem(lax.axis_index("gx"), 2) == 0
+    for buffer, east in ((side_a, even_x), (side_b, jnp.logical_not(even_x))):
+        first = jnp.where(east, 8 - EARLY, 0)
+        for d in range(EARLY):
+            for f in range(12):
+                at = (d * 12 + f) * 8
+                tile = start[f, first + d] if f < NC else perms[f - 9][first + d]
+                buffer[at : at + 8, :] = tile
+        first = jnp.where(east, 8 - LATE, 0)
+        for d in range(LATE):
+            for c in range(NC):
+                at = SIDE_RATIO + (d * NC + c) * 8
+                base = pl.multiple_of((c * 8 + d + first) * 8, 8)
+                buffer[at : at + 8, :] = ratio[pl.ds(base, 8), :]
 
 
 def shade_kernel(
@@ -308,8 +352,8 @@
     ratio,
     recv_a,
     recv_b,
-    edge_a,
-    edge_b,
+    side_a,
+    side_b,
     wide_hbm,
     send_a_hbm,
     send_b_hbm,
@@ -368,22 +412,26 @@
         first = jnp.where(east, 8 - EARLY, 0)
         for f in range(12):
             for d in range(EARLY):
-                at = (d * 12 + f) * 24
-                buffer[at : at + 24, :] = wide[first + d, f]
+                at = (d * 12 + f) * 16
+                buffer[at : at + 8, :] = wide[first + d, f, 0:8, :]
+                buffer[at + 8 : at + 16, :] = wide[first + d, f, 16:24, :]
         first = jnp.where(east, 8 - LATE, 0)
         for d in range(LATE):
             for c in range(NC):
-                at = RATIO_AT + (d * NC + c) * 16
-                buffer[at : at + 8, :] = wide[first + d, 12 + c, 8:16, :]
-                buffer[at + 8 : at + 16, :] = jnp.where(
+                at = CORNER_RATIO + (d * NC + c) * 8
+                buffer[at : at + 8, :] = jnp.where(
                     row < 4, wide[first + d, 12 + c, 16:24, :], wide[first + d, 12 + c, 0:8, :]
                 )
     for n, (source, target) in enumerate(((send_a, send_a_hbm), (send_b, send_b_hbm))):
         moves.append(pltpu.make_async_copy(source, target, sems_out.at[1 + n]))
         moves[-1].start()
     gx = lax.axis_index("gx")
-    px_west = jnp.where(even_x, edge_b[...], edge_a[...]) * (gx > 0).astype(F32)
-    px_east = jnp.where(even_x, edge_a[...], edge_b[...]) * (gx < 7).astype(F32)
+    west_at = slice(((EARLY - 1) * 12 + 9) * 8, ((EARLY - 1) * 12 + 10) * 8)
+    east_at = slice(9 * 8, 10 * 8)
+    px_west = jnp.where(even_x, side_b[west_at, :], side_a[west_at, :])
+    px_west = px_west * (gx > 0).astype(F32)
+    px_east = jnp.where(even_x, side_a[east_at, :], side_b[east_at, :])
+    px_east = px_east * (gx < 7).astype(F32)
     lane = lanes_of()
     totals = []
     for x in range(8):
@@ -423,7 +471,20 @@
 
 
 def early_kernel(
-    wide_hbm, recv_a, recv_b, trans, gain, begin, begin_edge, iters, perms, ratios, wide, sem
+    wide_hbm,
+    side_a,
+    side_b,
+    corner_a,
+    corner_b,
+    trans,
+    gain,
+    begin,
+    begin_edge,
+    iters,
+    perms,
+    ratios,
+    wide,
+    sem,
 ):
     copy = pltpu.make_async_copy(wide_hbm, wide, sem)
     copy.start()
@@ -434,30 +495,37 @@
     west_in = (gx > 0).astype(F32)
     east_in = (gx < 7).astype(F32)
 
+    def both(ref_a, ref_b, at, size):
+        at = pl.multiple_of(at, 8)
+        from_a = ref_a[pl.ds(at, size), :]
+        from_b = ref_b[pl.ds(at, size), :]
+        return jnp.where(even, from_b, from_a), jnp.where(even, from_a, from_b)
+
     def bring(d, _):
         for f in range(12):
-            at = pl.multiple_of((d * 12 + f) * 24, 8)
-            from_a = recv_a[pl.ds(at, 24), :]
-            from_b = recv_b[pl.ds(at, 24), :]
-            west = jnp.where(even, from_b, from_a)
-            east = jnp.where(even, from_a, from_b)
-            if f < NC:
-                iters[d, f] = west
-                iters[8 + EARLY + d, f] = east
-            else:
-                perms[d, f - 9] = west * west_in
-                perms[8 + EARLY + d, f - 9] = east * east_in
+            homes = both(side_a, side_b, (d * 12 + f) * 8, 8)
+            souths = both(corner_a, corner_b, (d * 12 + f) * 16, 8)
+            norths = both(corner_a, corner_b, (d * 12 + f) * 16 + 8, 8)
+            for side, inside in ((0, west_in), (1, east_in)):
+                here = d if side == 0 else 8 + EARLY + d
+                for t, tiles in enumerate((souths, homes, norths)):
+                    part = slice(8 * t, 8 * t + 8)
+                    if f < NC:
+                        iters[here, f, part, :] = tiles[side]
+                    else:
+                        perms[here, f - 9, part, :] = tiles[side] * inside
         return 0
 
     lax.fori_loop(0, EARLY, bring, 0)
 
     def bring_ratio(d, _):
         for c in range(NC):
-            at = pl.multiple_of(RATIO_AT + (d * NC + c) * 16, 8)
-            from_a = recv_a[pl.ds(at, 16), :]
-            from_b = recv_b[pl.ds(at, 16), :]
-            ratios[d, c] = jnp.where(even, from_b, from_a)
-            ratios[LATE + d, c] = jnp.where(even, from_a, from_b)
+            homes = both(side_a, side_b, SIDE_RATIO + (d * NC + c) * 8, 8)
+            outers = both(corner_a, corner_b, CORNER_RATIO + (d * NC + c) * 8, 8)
+            for side in range(2):
+                here = d if side == 0 else LATE + d
+                ratios[here, c, 0:8, :] = homes[side]
+                ratios[here, c, 8:16, :] = outers[side]
         return 0
 
     lax.fori_loop(0, LATE, bring_ratio, 0)
@@ -555,6 +623,8 @@
     weight,
     send_a,
     send_b,
+    side_a,
+    side_b,
     left,
     right,
     scale,
@@ -631,6 +701,13 @@
         at = slice(8 + i * LATE, 8 + i * LATE + LATE)
         send_a[at, :] = jnp.where(even, high, low)
         send_b[at, :] = jnp.where(even, low, high)
+    even_x = lax.rem(lax.axis_index("gx"), 2) == 0
+    for buffer, east in ((side_a, even_x), (side_b, jnp.logical_not(even_x))):
+        first = jnp.where(east, 8 - LATE, 0)
+        for d in range(LATE):
+            for c in range(NC):
+                at = pl.multiple_of((c * 8 + d + first) * 8, 8)
+                buffer[d, c] = weight[pl.ds(at, 8), :]
 
 
 def late_wide_kernel(weight, recv_a, recv_b, wide, edge, send_a, send_b):
@@ -652,25 +729,40 @@
         first = jnp.where(east, 8 - LATE, 0)
         for d in range(LATE):
             for c in range(NC):
-                buffer[d, c] = wide[first + d, c]
+                buffer[d, c] = wide[first + d, c, 8:16, :]
 
 
 def sweep_kernel(
-    trans, gain, begin, begin_edge, wide, edge, recv_a, recv_b, result, weight, one, two, last_one, sems
+    trans,
+    gain,
+    begin,
+    begin_edge,
+    wide,
+    edge,
+    side_a,
+    side_b,
+    corner_a,
+    corner_b,
+    result,
+    weight,
+    one,
+    two,
+    last_one,
+    sems,
 ):
     row = rows_of()
     even = lax.rem(lax.axis_index("gx"), 2) == 0
 
     def bring(d, _):
         for c in range(NC):
-            from_a = recv_a[d, c]
-            from_b = recv_b[d, c]
-            west = jnp.where(even, from_b, from_a)
-            east = jnp.where(even, from_a, from_b)
-            weight[d, c] = west
-            weight[8 + LATE + d, c] = east
-            one[d, c] = west + begin[d, c]
-            one[8 + LATE + d, c] = east + begin[8 + LATE + d, c]
+            for t, (ref_a, ref_b) in enumerate(((side_a, side_b), (corner_a, corner_b))):
+                part = slice(8 * t, 8 * t + 8)
+                west = jnp.where(even, ref_b[d, c], ref_a[d, c])
+                east = jnp.where(even, ref_a[d, c], ref_b[d, c])
+                weight[d, c, part, :] = west
+                weight[8 + LATE + d, c, part, :] = east
+                one[d, c, part, :] = west + begin[d, c, part, :]
+                one[8 + LATE + d, c, part, :] = east + begin[8 + LATE + d, c, part, :]
         return 0
 
     lax.fori_loop(0, LATE, bring, 0)
@@ -716,13 +808,20 @@
         return pltpu.make_async_copy(last_one.at[x], result.at[:, x], sems.at[x])
 
     def sweep(begin_at, end_at, held, new, brim=False, final=False):
-        def body(at, _):
-            column(at, held, new, brim, final)
-            if final:
-                writing(at - LATE).start()
+        count = end_at - begin_at
+        whole = count // 8 * 8
+
+        def run(at, size):
+            for step in range(size):
+                column(at + step, held, new, brim, final)
+                if final:
+                    writing(at + step - LATE).start()
             return 0
 
-        lax.fori_loop(begin_at, end_at, body, 0)
+        if whole:
+            lax.fori_loop(0, whole // 8, lambda i, _: run(begin_at + i * 8, 8), 0)
+        if count > whole:
+            lax.fori_loop(0, 1, lambda i, _: run(begin_at + whole + i, count - whole), 0)
 
     sweep(1, LATE, one, two)
     sweep(LATE, LATE + 8, one, two, brim=True)
@@ -736,10 +835,23 @@
 
 
 def swap_pairs(shards, axis):
-    count = lax.axis_size(axis)
-    inner = [(i, i ^ 1) for i in range(count)]
-    outer = [(i, (((i + 1) ^ 1) - 1) % count) for i in range(count)]
-    return lax.ppermute(shards[0], axis, inner), lax.ppermute(shards[1], axis, outer)
+    axes = ("gx", "gy")
+    sizes = [lax.axis_size(name) for name in axes]
+    along = axes.index(axis)
+    inner, outer = [], []
+    for i in range(sizes[0]):
+        for j in range(sizes[1]):
+            place = [i, j]
+            near, far_one = list(place), list(place)
+            near[along] = place[along] ^ 1
+            if along == 0 or 0 < place[1] < sizes[1] - 1:
+                far_one[along] = (((place[along] + 1) ^ 1) - 1) % sizes[along]
+            else:
+                far_one[0] = i ^ 1
+            here = i * sizes[1] + j
+            inner.append((here, near[0] * sizes[1] + near[1]))
+            outer.append((here, far_one[0] * sizes[1] + far_one[1]))
+    return lax.ppermute(shards[0], axes, inner), lax.ppermute(shards[1], axes, outer)
 
 
 def body(
@@ -771,69 +883,79 @@
         pltpu.VMEM((NC * 64, 128), BF16),
     ]
     given = [pin(x) for x in (start_iterate, perm_x, perm_y, perm_z, accum, mobil)]
-    mats, vecs, head, ratio, early_a, early_b, edge_a, edge_b = call(
+    mats, vecs, head, ratio, early_a, early_b, side_a, side_b = call(
         first_kernel,
         (
             out(81, 8, 128),
             out(NC, 8, 128),
-            out(BRICKS, 8, 128),
+            far(BRICKS, 8, 128),
             out(NC * 64, 128),
-            out(EARLY_ROWS, 128),
-            out(EARLY_ROWS, 128),
-            out(8, 128),
-            out(8, 128),
+            far(EARLY_ROWS, 128),
+            far(EARLY_ROWS, 128),
+            far(SIDE_ROWS, 128),
+            far(SIDE_ROWS, 128),
         ),
         [
             pltpu.VMEM((90, 8, 128), F32),
+            pltpu.VMEM((BRICKS, 8, 128), F32),
+            pltpu.VMEM((EARLY_ROWS, 128), F32),
+            pltpu.VMEM((EARLY_ROWS, 128), F32),
+            pltpu.VMEM((SIDE_ROWS, 128), F32),
+            pltpu.VMEM((SIDE_ROWS, 128), F32),
             pltpu.SMEM((8,), I32),
             pltpu.VMEM((NC, 8, 128), F32),
             pltpu.VMEM((NC, NC, 8, 128), F32),
             pltpu.VMEM((NC, NC, 8, 128), F32),
         ]
         + held
-        + [pltpu.SemaphoreType.DMA((10,))],
+        + [pltpu.SemaphoreType.DMA((10,)), pltpu.SemaphoreType.DMA((5,))],
         [HBM] * 10,
         "first",
         10_000_000,
+        out_specs=(VMEM, VMEM, HBM, VMEM, HBM, HBM, HBM, HBM),
     )(pin(well_len), pin(seg_source), pin(seg_inverse), pin(seg_outflow), *given)
     heads = lax.all_to_all(head, "gy", 0, 0, tiled=True)
     early_a, early_b = swap_pairs((early_a, early_b), "gy")
-    edge_a, edge_b = swap_pairs((edge_a, edge_b), "gx")
-
+
+    side_a, side_b = swap_pairs((side_a, side_b), "gx")
     lam, sent, token = call(
         rows_kernel,
-        (far(NC, 8, 128), far(BRICKS * SLOT, 128), out(8, 128)),
+        (
+            far(NC, 8, 128),
+            far(BRICKS * SLOT, 128),
+            out(8, 128),
+        ),
         [
             pltpu.VMEM((NC, 8, 128), F32),
             pltpu.VMEM((BRICKS * SLOT, 128), F32),
             pltpu.SMEM((BRICKS,), I32),
             pltpu.VMEM((BRICKS, 256), I32),
+            pltpu.VMEM((NC, NC, BRICKS, 256), F32),
             pltpu.SemaphoreType.DMA,
-            pltpu.SemaphoreType.DMA((2,)),
+            pltpu.SemaphoreType.DMA((3,)),
             pltpu.SemaphoreType.DMA((2,)),
         ],
-        [HBM, HBM] + [VMEM] * 6,
+        [HBM] * 3 + [VMEM] * 3,
         "well_rows",
+        20_000_000_000,
         out_specs=(HBM, HBM, VMEM),
     )(
         pin(perf_count.reshape(BRICKS)),
         pin(perf_seg.reshape(BRICKS, 256)),
+        pin(perf_coupling.reshape(NC, NC, BRICKS, 256)),
         mats,
         vecs,
         heads,
-        perf_coupling.reshape(NC, NC, BRICKS, 256),
-        edge_a,
-        edge_b,
     )
     arrived = lax.all_to_all(sent, "gy", 0, 0, tiled=True)
 
     cell = recv_cell.reshape(BRICKS, 2, 128)
-    wide, wide_a, wide_b, scale, base = call(
+    wide, corner_a, corner_b, scale, base = call(
         shade_kernel,
         (
             far(8, FIELDS, 24, 128),
-            far(WIDE_ROWS, 128),
-            far(WIDE_ROWS, 128),
+            far(CORNER_ROWS, 128),
+            far(CORNER_ROWS, 128),
             far(NC * 64, 128),
             far(NC * 64, 128),
         ),
@@ -841,8 +963,8 @@
         + [
             pltpu.VMEM((NC * 64, 128), BF16),
             pltpu.VMEM((8, FIELDS, 24, 128), F32),
-            pltpu.VMEM((WIDE_ROWS, 128), F32),
-            pltpu.VMEM((WIDE_ROWS, 128), F32),
+            pltpu.VMEM((CORNER_ROWS, 128), F32),
+            pltpu.VMEM((CORNER_ROWS, 128), F32),
             pltpu.VMEM((NC * 64, 128), F32),
             pltpu.VMEM((NC * 64, 128), F32),
             pltpu.SemaphoreType.DMA((7,)),
@@ -852,12 +974,18 @@
         "shade",
         limit=12,
         out_specs=(HBM,) * 5,
-    )(token, *given, pin(cot), ratio, early_a, early_b, edge_a, edge_b)
-    wide_a, wide_b = swap_pairs((wide_a, wide_b), "gx")
-
-    weight, late_a, late_b = call(
+    )(token, *given, pin(cot), ratio, early_a, early_b, side_a, side_b)
+    corner_a, corner_b = swap_pairs((corner_a, corner_b), "gx")
+
+    weight, late_a, late_b, late_side_a, late_side_b = call(
         scatter_kernel,
-        (out(NC * 64, 128), out(LATE_ROWS, 128), out(LATE_ROWS, 128)),
+        (
+            out(NC * 64, 128),
+            out(LATE_ROWS, 128),
+            out(LATE_ROWS, 128),
+            out(LATE, NC, 8, 128),
+            out(LATE, NC, 8, 128),
+        ),
         [
             pltpu.VMEM((288, 4096), BF16),
             pltpu.VMEM((512, 4096), BF16),
@@ -871,6 +999,7 @@
         limit=16,
     )(cell, arrived.reshape(BRICKS, SLOT, 128), pin(scale), pin(base))
     late_a, late_b = swap_pairs((late_a, late_b), "gy")
+    late_side_a, late_side_b = swap_pairs((late_side_a, late_side_b), "gx")
 
     trans, gain, begin, begin_edge = call(
         early_kernel,
@@ -887,24 +1016,24 @@
             pltpu.VMEM((8, FIELDS, 24, 128), F32),
             pltpu.SemaphoreType.DMA,
         ],
-        [HBM, VMEM, VMEM],
+        [HBM] + [VMEM] * 4,
         "early",
         limit=10,
-    )(pin(wide), wide_a, wide_b)
-
-    widened, edge, side_a, side_b = call(
+    )(pin(wide), side_a, side_b, corner_a, corner_b)
+
+    widened, edge, late_corner_a, late_corner_b = call(
         late_wide_kernel,
         (
             out(8, NC, 16, 128),
             out(8, NC, 8, 128),
-            out(LATE, NC, 16, 128),
-            out(LATE, NC, 16, 128),
+            out(LATE, NC, 8, 128),
+            out(LATE, NC, 8, 128),
         ),
         [],
         [VMEM] * 3,
         "late_wide",
     )(weight, late_a, late_b)
-    side_a, side_b = swap_pairs((side_a, side_b), "gx")
+    late_corner_a, late_corner_b = swap_pairs((late_corner_a, late_corner_b), "gx")
 
     wide_field = pltpu.VMEM((COLS, NC, 16, 128), F32)
     result = call(
@@ -912,10 +1041,21 @@
         out(NC, 8, 8, 128),
         [wide_field] * 3
         + [pltpu.VMEM((8, NC, 8, 128), F32), pltpu.SemaphoreType.DMA((8,))],
-        [VMEM] * 8,
+        [VMEM] * 10,
         "sweeps",
         out_specs=HBM,
-    )(trans, gain, begin, begin_edge, widened, edge, side_a, side_b)
+    )(
+        trans,
+        gain,
+        begin,
+        begin_edge,
+        widened,
+        edge,
+        late_side_a,
+        late_side_b,
+        late_corner_a,
+        late_corner_b,
+    )
     return lam, result
 
 

time: 74.2 us -> 60.5 us (0.82)
  starting transfers between devices: 30.8 us -> 25.2 us
  Pallas kernels: 29.4 us -> 24.2 us
  waiting for transfers between devices: 12.5 us -> 9.94 us
    ppermute x10 -> x12, starting transfers between devices: 23.8 us -> 12.3 us  [the longest x6 8.54 us: swap_pairs(): lax.ppermute(shards[1], axes, outer)]
    all_to_all x1, starting transfers between devices: 3.5 us -> 7.13 us  [body(): heads = lax.all_to_all(head, 'gy', 0, 0, tiled=True)]
    pallas_call x1, Pallas kernels: 7.46 us -> 3.92 us  [body(): call(sweep_kernel, out(NC, 8, 8, 128), [wide_field] * 3 + [pltpu.VMEM((8,...]
    all_to_all x1, waiting for transfers between devices: 5.24 us -> 1.83 us  [body(): heads = lax.all_to_all(head, 'gy', 0, 0, tiled=True)]
    all_to_all x1, waiting for transfers between devices: 0.21 us -> 2.81 us  [body(): arrived = lax.all_to_all(sent, 'gy', 0, 0, tiled=True)]
    all_to_all x1, starting transfers between devices: 3.53 us -> 5.81 us  [body(): arrived = lax.all_to_all(sent, 'gy', 0, 0, tiled=True)]
    ppermute x10 -> x12, waiting for transfers between devices: 7.06 us -> 5.3 us  [the longest x6 4.56 us: swap_pairs(): lax.ppermute(shards[0], axes, inner)]
    pallas_call x2, Pallas kernels: 9.5 us -> 8.48 us  [the longest x1 4.98 us: body(): call(first_kernel, (out(81, 8, 128), out(NC, 8, 128), far(BRICKS, 8, 128)...]
  transfers between devices with their start and end apart: 12 -> 14, of which waited for: 5 -> 4; matrix products, arithmetic and copies ran while one was open for 0% -> 0% of each run, Pallas kernels for 22% -> 25%
where the time goes in v2:
time: 60.5 us; the launch traced here: 60.2 us
  starting transfers between devices  25.2 us (42%)
  Pallas kernels  24.2 us (40%)
  waiting for transfers between devices  9.94 us (16%)
  between operations  0.79 us (1%)
    ppermute x6, starting transfers between devices, swap_pairs(): lax.ppermute(shards[1], axes, outer)  8.54 us
    all_to_all x1, starting transfers between devices, body(): heads = lax.all_to_all(head, 'gy', 0, 0, tiled=True)  7.13 us
    all_to_all x1, starting transfers between devices, body(): arrived = lax.all_to_all(sent, 'gy', 0, 0, tiled=True)  5.81 us
    pallas_call x1, Pallas kernels, body(): call(first_kernel, (out(81, 8, 128), out(NC, 8, 128), far(BRICKS, 8, 128)...  4.98 us
    ppermute x6, waiting for transfers between devices, swap_pairs(): lax.ppermute(shards[0], axes, inner)  4.56 us
    pallas_call x1, Pallas kernels, body(): call(early_kernel, (out(COLS, 6, 16, 128), out(COLS, NC, 16, 128), out(CO...  4.13 us
    pallas_call x1, Pallas kernels, body(): call(sweep_kernel, out(NC, 8, 8, 128), [wide_field] * 3 + [pltpu.VMEM((8,...  3.92 us
    pallas_call x1, Pallas kernels, body(): call(rows_kernel, (far(NC, 8, 128), far(BRICKS * SLOT, 128), out(8, 128))...  3.77 us
  transfers between devices with their start and end apart: 14, of which 4 were waited for; matrix products, arithmetic and copies ran while one was open for 0% of the time, Pallas kernels for 25%

profile of v2, /device:TPU:0, one launch (start us, length us, event | category | flops | bytes accessed | tf_op | source)
XLA Modules:
  0.0 60.2 jit_solution(1913184698547569288)
XLA Ops:
  0.6 5.0 %first.1 = (f32[81,8,128]{2,1,0:T(8,128)S(1)}, f32[9,8,128]{2,1,0:T(8,128)S(1)}, f32[16,8,128]{2,1,0:T(8,128)}, f32[576,128]{1,0:T(8,128)S(1)}, f32[1024,128]{1,...) custom-call(s32[8]{0:T(128)} %len_hbm.1, f32[9,8,128]{2,1,0:T(8,128)} %src_hbm.1, ...), custom_call_target="tpu_custom_call" | custom-call | flops 10000000 | bytes 1000000 | tf_op jit(solution)/shard_map/first/pallas_call | solution.py:886
  5.6 7.1 %all-to-all-start = ((f32[16,8,128]{2,1,0:T(8,128)}), f32[16,8,128]{2,1,0:T(8,128)S(1)}, u32[]{:S(2)}, u32[]{:S(2)}) async-start(f32[16,8,128]{2,1,0:T(8,128)} %get-tuple-element.33), calls=%async_computation | async-start | bytes 131072 | tf_op jit(solution)/shard_map/all_to_all | solution.py:917
  12.8 1.9 %collective-permute-start = (f32[1024,128]{1,0:T(8,128)}, f32[1024,128]{1,0:T(8,128)S(1)}, u32[]{:S(2)}, u32[]{:S(2)}) collective-permute-start(f32[1024,128]{1,0:T(8,128)} %get-tuple-element.37), channel_id=1, source_target_pairs={{0,1},{1,0},{2,3},{3,2},{4,5},{5,4},{6,7},{7,6},{8,9},{9,8},{10,11... | collective-permute-start | bytes 1572872 | tf_op jit(solution)/shard_map/ppermute | solution.py:854
  14.7 0.0 collective-permute-start.1
  14.7 0.5 collective-permute-start.2
  15.2 3.6 %collective-permute-start.3 = (f32[936,128]{1,0:T(8,128)}, f32[936,128]{1,0:T(8,128)S(1)}, u32[]{:S(2)}, u32[]{:S(2)}) collective-permute-start(f32[936,128]{1,0:T(8,128)} %get-tuple-element.40), channel_id=1, source_target_pairs={{0,112},{1,113},{2,114},{3,115},{4,116},{5,117},{6,118},{7,119},{8... | collective-permute-start | bytes 1437704 | tf_op jit(solution)/shard_map/ppermute | solution.py:854
  18.8 1.8 %all-to-all-done.heads = f32[16,8,128]{2,1,0:T(8,128)S(1)} async-done(((f32[16,8,128]{2,1,0:T(8,128)}), f32[16,8,128]{2,1,0:T(8,128)S(1)}, u32[]{:S(2)}, u32[]{:S(2)}) %all-to-all-start) | async-done | bytes 65568 | tf_op jit(solution)/shard_map/all_to_all | solution.py:917
  20.7 3.8 %well_rows.1 = (f32[9,8,128]{2,1,0:T(8,128)}, f32[384,128]{1,0:T(8,128)}, f32[8,128]{1,0:T(8,128)S(1)}) custom-call(s32[16]{0:T(128)} %bitcast.17, s32[16,256]{1,0:T(8,128)} %bitcast.16, f32[9,9,16,256]{3,2,1,0:T(8,128)} %bitcast.15, f32[81,8,128]{2,1,0:T(8,128)S(1)} %get-tuple-element.31.mats, f32[9,8,128]{2,1,0:T(8,128)S(1)} %get-tuple-element.32.vecs, ...), custom_call_target="tpu_custom_call" | custom-call | flops 20000000000 | bytes 1000000 | tf_op jit(solution)/shard_map/well_rows/pallas_call | solution.py:921
  24.5 5.8 %all-to-all-start.1 = ((f32[16,24,128]{2,1,0:T(8,128)}), f32[16,24,128]{2,1,0:T(8,128)S(1)}, u32[]{:S(2)}, u32[]{:S(2)}) async-start(f32[16,24,128]{2,1,0:T(8,128)} %bitcast.13), calls=%async_computation.1 | async-start | bytes 393216 | tf_op jit(solution)/shard_map/all_to_all | solution.py:950
  30.3 0.0 collective-permute-done.2.side_a
  30.3 0.0 collective-permute-done.3.side_b
  30.3 0.0 collective-permute-done.1.recv_b
  30.3 3.5 %shade.1 = (f32[8,21,24,128]{3,2,1,0:T(8,128)}, f32[1512,128]{1,0:T(8,128)}, f32[1512,128]{1,0:T(8,128)}, f32[576,128]{1,0:T(8,128)}, f32[576,128]{1,0:T(8,128)}) custom-call(f32[8,128]{1,0:T(8,128)S(1)} %get-tuple-element.35.after, f32[9,8,8,128]{3,2,1,0:T(8,128)} %start_hbm.3, f32[8,8,128]{2,1,0:T(8,128)} %px_hbm.3, f32[8,8,128]{2,1,0:T(8,128)} %py_hbm.3, ...), custom_call_target="tpu_custom_call" | custom-call | flops 1000000 | bytes 1000000 | tf_op jit(solution)/shard_map/shade/pallas_call | solution.py:953
  33.9 0.1 collective-permute-start.4
  33.9 1.9 %collective-permute-start.5 = (f32[1512,128]{1,0:T(8,128)}, f32[1512,128]{1,0:T(8,128)S(1)}, u32[]{:S(2)}, u32[]{:S(2)}) collective-permute-start(f32[1512,128]{1,0:T(8,128)} %get-tuple-element.43), channel_id=1, source_target_pairs={{0,112},{1,113},{2,114},{3,115},{4,116},{5,117},{6,118},{7,119},{8... | collective-permute-start | bytes 2322440 | tf_op jit(solution)/shard_map/ppermute | solution.py:854
  35.8 2.8 %all-to-all-done.1.arrived = f32[16,24,128]{2,1,0:T(8,128)S(1)} async-done(((f32[16,24,128]{2,1,0:T(8,128)}), f32[16,24,128]{2,1,0:T(8,128)S(1)}, u32[]{:S(2)}, u32[]{:S(2)}) %all-to-all-start.1) | async-done | bytes 196640 | tf_op jit(solution)/shard_map/all_to_all | solution.py:950
  38.6 3.8 %scatter.1 = (f32[576,128]{1,0:T(8,128)S(1)}, f32[376,128]{1,0:T(8,128)S(1)}, f32[376,128]{1,0:T(8,128)S(1)}, f32[5,9,8,128]{3,2,1,0:T(8,128)S(1)}, f32[5,9,8,128]{3,2,1,0:T(8,128)S(1)}) custom-call(s32[16,2,128]{2,1,0:T(2,128)S(1)} %reshape.35.cell, f32[16,24,128]{2,1,0:T(8,128)S(1)} %all-to-all-done.1.arrived, f32[576,128]{1,0:T(8,128)} %get-tuple-element.49.scale_hbm, ...), custom_call_target="tpu_custom_call" | custom-call | flops 20000000000 | bytes 1000000 | tf_op jit(solution)/shard_map/scatter/pallas_call | solution.py:980
  42.4 0.6 %collective-permute-start.6 = (f32[376,128]{1,0:T(8,128)S(1)}, f32[376,128]{1,0:T(8,128)S(1)}, u32[]{:S(2)}, u32[]{:S(2)}) collective-permute-start(f32[376,128]{1,0:T(8,128)S(1)} %get-tuple-element.52), channel_id=1, source_target_pairs={{0,1},{1,0},{2,3},{3,2},{4,5},{5,4},{6,7},{7,6},{8,9},{9,8},{10,11... | collective-permute-start | bytes 577544 | tf_op jit(solution)/shard_map/ppermute | solution.py:854
  43.0 0.0 collective-permute-start.7
  43.0 0.5 collective-permute-start.8
  43.5 4.6 %collective-permute-done.6.recv_a = f32[376,128]{1,0:T(8,128)S(1)} collective-permute-done((f32[376,128]{1,0:T(8,128)S(1)}, f32[376,128]{1,0:T(8,128)S(1)}, u32[]{:S(2)}, u32[]{:S(2)}) %collective-permute-start.6) | collective-permute-done | bytes 192544 | tf_op jit(solution)/shard_map/ppermute | solution.py:854
  48.1 0.0 collective-permute-start.9
  48.1 0.0 collective-permute-done.7.recv_b
  48.1 0.1 late_wide.1
  48.2 0.1 collective-permute-start.10
  48.3 0.0 collective-permute-done.4.corner_a
  48.3 3.0 %collective-permute-start.11 = (f32[5,9,8,128]{3,2,1,0:T(8,128)S(1)}, f32[5,9,8,128]{3,2,1,0:T(8,128)S(1)}, u32[]{:S(2)}, u32[]{:S(2)}) collective-permute-start(f32[5,9,8,128]{3,2,1,0:T(8,128)S(1)} %get-tuple-element.59), channel_id=1, source_target_pairs={{0,112},{1,113},{2,114},{3,115},{4,116},{5,117},{6,118},{7,119},{8... | collective-permute-start | bytes 552968 | tf_op jit(solution)/shard_map/ppermute | solution.py:854
  51.4 0.0 collective-permute-done.5.corner_b
  51.4 4.1 %early.1 = (f32[18,6,16,128]{3,2,1,0:T(8,128)S(1)}, f32[18,9,16,128]{3,2,1,0:T(8,128)S(1)}, f32[18,9,16,128]{3,2,1,0:T(8,128)S(1)}, f32[8,9,8,128]{3,2,1,0:T(8,128)S(1)}) custom-call(f32[8,21,24,128]{3,2,1,0:T(8,128)} %get-tuple-element.41.wide_hbm, f32[936,128]{1,0:T(8,128)S(1)} %collective-permute-done.2.side_a, ...), custom_call_target="tpu_custom_call" | custom-call | flops 1000000 | bytes 1000000 | tf_op jit(solution)/shard_map/early/pallas_call | solution.py:1004
  55.5 0.0 collective-permute-done.8.side_a
  55.5 0.7 %collective-permute-done.11.corner_b = f32[5,9,8,128]{3,2,1,0:T(8,128)S(1)} collective-permute-done((f32[5,9,8,128]{3,2,1,0:T(8,128)S(1)}, f32[5,9,8,128]{3,2,1,0:T(8,128)S(1)}, u32[]{:S(2)}, u32[]{:S(2)}) %collective-permute-start.11) | collective-permute-done | bytes 184352 | tf_op jit(solution)/shard_map/ppermute | solution.py:854
  56.2 3.9 %sweeps.1 = f32[9,8,8,128]{3,2,1,0:T(8,128)} custom-call(f32[18,6,16,128]{3,2,1,0:T(8,128)S(1)} %get-tuple-element.44.trans, f32[18,9,16,128]{3,2,1,0:T(8,128)S(1)} %get-tuple-element.45.gain, f32[18,9,16,128]{3,2,1,0:T(8,128)S(1)} %get-tuple-element.46.begin, f32[8,9,8,128]{3,2,1,0:T(8,128)S(1)} %get-tuple-element.47.begin_edge, ...), custom_call_target="tpu_custom_call" | custom-call | flops 1000000 | bytes 1000000 | tf_op jit(solution)/shard_map/sweeps/pallas_call | solution.py:1039
  (6 shorter events, 0.0 us)
Async XLA Ops:
  5.6 15.1 %all-to-all-start = ((f32[16,8,128]{2,1,0:T(8,128)}), f32[16,8,128]{2,1,0:T(8,128)S(1)}, u32[]{:S(2)}, u32[]{:S(2)}) async-start(f32[16,8,128]{2,1,0:T(8,128)} %get-tuple-element.33), calls=%async_computation | async-start | bytes 131072 | tf_op jit(solution)/shard_map/all_to_all | solution.py:917
  12.8 17.6 %collective-permute-start = (f32[1024,128]{1,0:T(8,128)}, f32[1024,128]{1,0:T(8,128)S(1)}, u32[]{:S(2)}, u32[]{:S(2)}) collective-permute-start(f32[1024,128]{1,0:T(8,128)} %get-tuple-element.37), channel_id=1, source_target_pairs={{0,1},{1,0},{2,3},{3,2},{4,5},{5,4},{6,7},{7,6},{8,9},{9,8},{10,11... | collective-permute-start | bytes 1572872 | tf_op jit(solution)/shard_map/ppermute | solution.py:854
  14.7 15.7 %collective-permute-start.1 = (f32[1024,128]{1,0:T(8,128)}, f32[1024,128]{1,0:T(8,128)S(1)}, u32[]{:S(2)}, u32[]{:S(2)}) collective-permute-start(f32[1024,128]{1,0:T(8,128)} %get-tuple-element.38), channel_id=1, source_target_pairs={{0,16},{1,2},{2,1},{3,4},{4,3},{5,6},{6,5},{7,8},{8,7},{9,10},{10,... | collective-permute-start | bytes 1572872 | tf_op jit(solution)/shard_map/ppermute | solution.py:854
  14.7 15.6 %collective-permute-start.2 = (f32[936,128]{1,0:T(8,128)}, f32[936,128]{1,0:T(8,128)S(1)}, u32[]{:S(2)}, u32[]{:S(2)}) collective-permute-start(f32[936,128]{1,0:T(8,128)} %get-tuple-element.39), channel_id=1, source_target_pairs={{0,16},{1,17},{2,18},{3,19},{4,20},{5,21},{6,22},{7,23},{8,24},{9,... | collective-permute-start | bytes 1437704 | tf_op jit(solution)/shard_map/ppermute | solution.py:854
  15.2 15.1 %collective-permute-start.3 = (f32[936,128]{1,0:T(8,128)}, f32[936,128]{1,0:T(8,128)S(1)}, u32[]{:S(2)}, u32[]{:S(2)}) collective-permute-start(f32[936,128]{1,0:T(8,128)} %get-tuple-element.40), channel_id=1, source_target_pairs={{0,112},{1,113},{2,114},{3,115},{4,116},{5,117},{6,118},{7,119},{8... | collective-permute-start | bytes 1437704 | tf_op jit(solution)/shard_map/ppermute | solution.py:854
  20.7 9.6 %copy-start = (s32[1,1,16,256]{3,2,1,0:T(8,128)S(1)}, s32[1,1,16,256]{3,2,1,0:T(8,128)}, u32[]{:S(2)}) copy-start(s32[1,1,16,256]{3,2,1,0:T(8,128)} %param.22) | copy-start | bytes 49156
  24.5 14.2 %all-to-all-start.1 = ((f32[16,24,128]{2,1,0:T(8,128)}), f32[16,24,128]{2,1,0:T(8,128)S(1)}, u32[]{:S(2)}, u32[]{:S(2)}) async-start(f32[16,24,128]{2,1,0:T(8,128)} %bitcast.13), calls=%async_computation.1 | async-start | bytes 393216 | tf_op jit(solution)/shard_map/all_to_all | solution.py:950
  33.9 14.5 %collective-permute-start.4 = (f32[1512,128]{1,0:T(8,128)}, f32[1512,128]{1,0:T(8,128)S(1)}, u32[]{:S(2)}, u32[]{:S(2)}) collective-permute-start(f32[1512,128]{1,0:T(8,128)} %get-tuple-element.42), channel_id=1, source_target_pairs={{0,16},{1,17},{2,18},{3,19},{4,20},{5,21},{6,22},{7,23},{8,24},{9,... | collective-permute-start | bytes 2322440 | tf_op jit(solution)/shard_map/ppermute | solution.py:854
  33.9 17.4 %collective-permute-start.5 = (f32[1512,128]{1,0:T(8,128)}, f32[1512,128]{1,0:T(8,128)S(1)}, u32[]{:S(2)}, u32[]{:S(2)}) collective-permute-start(f32[1512,128]{1,0:T(8,128)} %get-tuple-element.43), channel_id=1, source_target_pairs={{0,112},{1,113},{2,114},{3,115},{4,116},{5,117},{6,118},{7,119},{8... | collective-permute-start | bytes 2322440 | tf_op jit(solution)/shard_map/ppermute | solution.py:854
  42.4 5.7 %collective-permute-start.6 = (f32[376,128]{1,0:T(8,128)S(1)}, f32[376,128]{1,0:T(8,128)S(1)}, u32[]{:S(2)}, u32[]{:S(2)}) collective-permute-start(f32[376,128]{1,0:T(8,128)S(1)} %get-tuple-element.52), channel_id=1, source_target_pairs={{0,1},{1,0},{2,3},{3,2},{4,5},{5,4},{6,7},{7,6},{8,9},{9,8},{10,11... | collective-permute-start | bytes 577544 | tf_op jit(solution)/shard_map/ppermute | solution.py:854
  43.0 5.1 %collective-permute-start.7 = (f32[376,128]{1,0:T(8,128)S(1)}, f32[376,128]{1,0:T(8,128)S(1)}, u32[]{:S(2)}, u32[]{:S(2)}) collective-permute-start(f32[376,128]{1,0:T(8,128)S(1)} %get-tuple-element.53), channel_id=1, source_target_pairs={{0,16},{1,2},{2,1},{3,4},{4,3},{5,6},{6,5},{7,8},{8,7},{9,10},{10,... | collective-permute-start | bytes 577544 | tf_op jit(solution)/shard_map/ppermute | solution.py:854
  43.0 12.5 %collective-permute-start.8 = (f32[5,9,8,128]{3,2,1,0:T(8,128)S(1)}, f32[5,9,8,128]{3,2,1,0:T(8,128)S(1)}, u32[]{:S(2)}, u32[]{:S(2)}) collective-permute-start(f32[5,9,8,128]{3,2,1,0:T(8,128)S(1)} %get-tuple-element.56), channel_id=1, source_target_pairs={{0,16},{1,17},{2,18},{3,19},{4,20},{5,21},{6,22},{7,23},{8,24},{9,... | collective-permute-start | bytes 552968 | tf_op jit(solution)/shard_map/ppermute | solution.py:854
  48.1 7.4 %collective-permute-start.9 = (f32[5,9,8,128]{3,2,1,0:T(8,128)S(1)}, f32[5,9,8,128]{3,2,1,0:T(8,128)S(1)}, u32[]{:S(2)}, u32[]{:S(2)}) collective-permute-start(f32[5,9,8,128]{3,2,1,0:T(8,128)S(1)} %get-tuple-element.57), channel_id=1, source_target_pairs={{0,112},{1,113},{2,114},{3,115},{4,116},{5,117},{6,118},{7,119},{8... | collective-permute-start | bytes 552968 | tf_op jit(solution)/shard_map/ppermute | solution.py:854
  48.2 7.3 %collective-permute-start.10 = (f32[5,9,8,128]{3,2,1,0:T(8,128)S(1)}, f32[5,9,8,128]{3,2,1,0:T(8,128)S(1)}, u32[]{:S(2)}, u32[]{:S(2)}) collective-permute-start(f32[5,9,8,128]{3,2,1,0:T(8,128)S(1)} %get-tuple-element.58), channel_id=1, source_target_pairs={{0,16},{1,17},{2,18},{3,19},{4,20},{5,21},{6,22},{7,23},{8,24},{9,... | collective-permute-start | bytes 552968 | tf_op jit(solution)/shard_map/ppermute | solution.py:854
  48.3 7.9 %collective-permute-start.11 = (f32[5,9,8,128]{3,2,1,0:T(8,128)S(1)}, f32[5,9,8,128]{3,2,1,0:T(8,128)S(1)}, u32[]{:S(2)}, u32[]{:S(2)}) collective-permute-start(f32[5,9,8,128]{3,2,1,0:T(8,128)S(1)} %get-tuple-element.59), channel_id=1, source_target_pairs={{0,112},{1,113},{2,114},{3,115},{4,116},{5,117},{6,118},{7,119},{8... | collective-permute-start | bytes 552968 | tf_op jit(solution)/shard_map/ppermute | solution.py:854

commit v3 on v2

--- a/solution.py
+++ b/solution.py
@@ -24,6 +24,7 @@
 CORNER_ROWS = CORNER_RATIO + NC * LATE * 8
 COLS = 8 + 2 * LATE
 SLOT = 24
+CHUNKS = 4
 
 VMEM = pl.BlockSpec(memory_space=pltpu.VMEM)
 SMEM = pl.BlockSpec(memory_space=pltpu.SMEM)
@@ -591,6 +592,13 @@
                 scale = OMEGA / (ratio[2] + edge(total))
                 begin_edge[at - LATE, c] = KEEP * edge(mid) + scale * edge(beside)
 
+    def pairs(body):
+        def run(i, _):
+            body(i * 2, 0)
+            return body(i * 2 + 1, 0)
+
+        return run
+
     def home_column(x, _):
         def ratio_of(c):
             south = wide[x, 12 + c, 0:8, :]
@@ -611,8 +619,8 @@
         column(jnp.where(d < LATE, d, d + 8), ratio_of)
         return 0
 
-    lax.fori_loop(0, 8, home_column, 0)
-    lax.fori_loop(0, 2 * LATE, halo_column, 0)
+    lax.fori_loop(0, 4, pairs(home_column), 0)
+    lax.fori_loop(0, LATE, pairs(halo_column), 0)
 
 
 def scatter_kernel(
@@ -625,8 +633,10 @@
     send_b,
     side_a,
     side_b,
-    left,
-    right,
+    left_one,
+    left_two,
+    right_one,
+    right_two,
     scale,
     base,
     sems,
@@ -638,58 +648,58 @@
     )
     row16 = rows_of((16, 128))
 
-    def mark(j, _):
+    row_mark = row16.astype(F32).astype(BF16)
+    nothing = jnp.bfloat16(0.0)
+
+    def mark(j, at_j, left, right):
         for half in range(2):
-            at = pl.ds(pl.multiple_of(j * 256 + half * 128, 128), 128)
+            at = slice(at_j * 256 + half * 128, at_j * 256 + half * 128 + 128)
             place = jnp.broadcast_to(cell[j, half : half + 1, :], (16, 128))
-            high = lax.bitwise_or(
-                lax.bitwise_and(place, 127),
-                lax.shift_left(lax.shift_right_logical(place, 11), 7),
+            block = lax.bitwise_or(
+                lax.bitwise_and(lax.shift_right_logical(place, 4), 7),
+                lax.shift_left(lax.shift_right_logical(place, 12), 3),
             )
-            for n in range(32):
+            block = block.astype(F32).astype(BF16)
+            mark16 = jnp.where(lax.bitwise_and(place, 15) == row16, 1.0, 0.0).astype(BF16)
+            for n in range(16):
                 right[n * 16 : n * 16 + 16, at] = jnp.where(
-                    high == row16 + n * 16, 1.0, 0.0
-                ).astype(BF16)
-        return 0
-
-    lax.fori_loop(0, BRICKS, mark, 0)
-    def build(j, _):
-        for half in range(2):
-            at = pl.ds(pl.multiple_of(j * 256 + half * 128, 128), 128)
-            place = cell[j, half : half + 1, :]
-            place = jnp.broadcast_to(place, (16, 128))
-            low = lax.bitwise_and(lax.shift_right_logical(place, 7), 15)
-            mine = low == row16
+                    block == jnp.bfloat16(n), mark16, nothing
+                )
+            low = lax.bitwise_and(lax.shift_right_logical(place, 7), 31)
+            low = low.astype(F32).astype(BF16)
+            mine = (low == row_mark, low == row_mark + jnp.bfloat16(16))
             values = arrived[j, pl.ds(half, NC, stride=2), :]
             coarse = values.astype(BF16).astype(F32)
             fine = values - coarse
             for c in range(NC):
                 for part, source in ((0, coarse), (1, fine)):
-                    line = jnp.broadcast_to(source[c : c + 1, :], (16, 128))
-                    left[part * 144 + c * 16 : part * 144 + c * 16 + 16, at] = jnp.where(
-                        mine, line, 0.0
-                    ).astype(BF16)
-        return 0
-
-    lax.fori_loop(0, BRICKS, build, 0)
-
-    for part in range(2):
-        if part == 0:
-            copies[0].wait()
-            copies[1].wait()
-        product = lax.dot_general(
-            left[...],
-            right[part * 256 : part * 256 + 256, :],
-            (((1,), (1,)), ((), ())),
-            preferred_element_type=F32,
-        )
+                    line = jnp.broadcast_to(source[c : c + 1, :], (16, 128)).astype(BF16)
+                    for t in range(2):
+                        first = part * 288 + c * 32 + t * 16
+                        left[first : first + 16, at] = jnp.where(mine[t], line, nothing)
+
+    size = BRICKS // CHUNKS
+    lefts, rights = (left_one, left_two), (right_one, right_two)
+    product = jnp.zeros((576, 256), F32)
+    for chunk in range(CHUNKS + 1):
+        if chunk < CHUNKS:
+            for n in range(size):
+                mark(chunk * size + n, n, lefts[chunk % 2], rights[chunk % 2])
+        if chunk > 0:
+            product = product + lax.dot_general(
+                lefts[(chunk - 1) % 2][...],
+                rights[(chunk - 1) % 2][...],
+                (((1,), (1,)), ((), ())),
+                preferred_element_type=F32,
+            )
+    for copy in copies:
+        copy.wait()
+    for c in range(NC):
         for side in range(2):
-            pair = part * 2 + side
             at = slice(side * 128, side * 128 + 128)
-            for c in range(NC):
-                well = product[c * 16 : c * 16 + 16, at] + product[144 + c * 16 : 160 + c * 16, at]
-                here = slice((c * 4 + pair) * 16, (c * 4 + pair) * 16 + 16)
-                weight[here, :] = base[here, :] - scale[here, :] * well
+            well = product[c * 32 : c * 32 + 32, at] + product[288 + c * 32 : 320 + c * 32, at]
+            here = slice((c * 2 + side) * 32, (c * 2 + side) * 32 + 32)
+            weight[here, :] = base[here, :] - scale[here, :] * well
 
     even = lax.rem(lax.axis_index("gy"), 2) == 0
     for buffer in (send_a, send_b):
@@ -726,10 +736,16 @@
             edge[x, c] = jnp.where(row == 4, north, south)
     even_x = lax.rem(lax.axis_index("gx"), 2) == 0
     for buffer, east in ((send_a, even_x), (send_b, jnp.logical_not(even_x))):
-        first = jnp.where(east, 8 - LATE, 0)
-        for d in range(LATE):
-            for c in range(NC):
-                buffer[d, c] = wide[first + d, c, 8:16, :]
+        first, step = jnp.where(east, 7, 0), jnp.where(east, -1, 1)
+        for c in range(NC):
+            one, two, three, four = (wide[first + n * step, c, 8:16, :] for n in range(4))
+            buffer[0, c] = one
+            buffer[1, c] = jnp.where(
+                row == 3,
+                pltpu.roll(four, 3, 0),
+                jnp.where(row == 4, pltpu.roll(four, 5, 0), two),
+            )
+            buffer[2, c] = three
 
 
 def sweep_kernel(
@@ -753,19 +769,24 @@
     row = rows_of()
     even = lax.rem(lax.axis_index("gx"), 2) == 0
 
-    def bring(d, _):
-        for c in range(NC):
-            for t, (ref_a, ref_b) in enumerate(((side_a, side_b), (corner_a, corner_b))):
-                part = slice(8 * t, 8 * t + 8)
-                west = jnp.where(even, ref_b[d, c], ref_a[d, c])
-                east = jnp.where(even, ref_a[d, c], ref_b[d, c])
-                weight[d, c, part, :] = west
-                weight[8 + LATE + d, c, part, :] = east
-                one[d, c, part, :] = west + begin[d, c, part, :]
-                one[8 + LATE + d, c, part, :] = east + begin[8 + LATE + d, c, part, :]
+    def place(at, c, part, tile):
+        weight[at, c, part, :] = tile
+        one[at, c, part, :] = tile + begin[at, c, part, :]
+
+    def bring(c, _):
+        home, outer = slice(0, 8), slice(8, 16)
+        for d in range(LATE):
+            place(d, c, home, jnp.where(even, side_b[d, c], side_a[d, c]))
+            place(8 + LATE + d, c, home, jnp.where(even, side_a[d, c], side_b[d, c]))
+        for near, ref_odd, ref_even in ((4, corner_a, corner_b), (13, corner_b, corner_a)):
+            step = -1 if near == 4 else 1
+            tiles = [jnp.where(even, ref_even[n, c], ref_odd[n, c]) for n in range(3)]
+            far_tile = jnp.where(row == 0, pltpu.roll(tiles[1], 5, 0), pltpu.roll(tiles[1], 3, 0))
+            for n, tile in enumerate((tiles[0], tiles[1], tiles[2], far_tile, far_tile)):
+                place(near + n * step, c, outer, tile)
         return 0
 
-    lax.fori_loop(0, LATE, bring, 0)
+    lax.fori_loop(0, NC, bring, 0)
 
     def settle(x, _):
         for c in range(NC):
@@ -987,8 +1008,10 @@
             out(LATE, NC, 8, 128),
         ),
         [
-            pltpu.VMEM((288, 4096), BF16),
-            pltpu.VMEM((512, 4096), BF16),
+            pltpu.VMEM((576, 4096 // CHUNKS), BF16),
+            pltpu.VMEM((576, 4096 // CHUNKS), BF16),
+            pltpu.VMEM((256, 4096 // CHUNKS), BF16),
+            pltpu.VMEM((256, 4096 // CHUNKS), BF16),
             pltpu.VMEM((NC * 64, 128), F32),
             pltpu.VMEM((NC * 64, 128), F32),
             pltpu.SemaphoreType.DMA((2,)),
@@ -1026,8 +1049,8 @@
         (
             out(8, NC, 16, 128),
             out(8, NC, 8, 128),
-            out(LATE, NC, 8, 128),
-            out(LATE, NC, 8, 128),
+            out(3, NC, 8, 128),
+            out(3, NC, 8, 128),
         ),
         [],
         [VMEM] * 3,

time: 60.5 us -> 59 us (0.975)
  Pallas kernels: 24.2 us -> 22.7 us
    pallas_call x1, Pallas kernels: 3.76 us -> 2.96 us  [body(): call(scatter_kernel, (out(NC * 64, 128), out(LATE_ROWS, 128), out(LATE_RO...]
  transfers between devices with their start and end apart: 14 -> 14, of which waited for: 4 -> 4; matrix products, arithmetic and copies ran while one was open for 0% -> 0% of each run, Pallas kernels for 25% -> 24%
where the time goes in v3:
time: 59 us; the launch traced here: 58.6 us
  starting transfers between devices  25.4 us (43%)
  Pallas kernels  22.7 us (38%)
  waiting for transfers between devices  9.52 us (16%)
  between operations  0.95 us (2%)
    ppermute x6, starting transfers between devices, swap_pairs(): lax.ppermute(shards[1], axes, outer)  8.72 us
    all_to_all x1, starting transfers between devices, body(): heads = lax.all_to_all(head, 'gy', 0, 0, tiled=True)  7.13 us
    all_to_all x1, starting transfers between devices, body(): arrived = lax.all_to_all(sent, 'gy', 0, 0, tiled=True)  5.81 us
    pallas_call x1, Pallas kernels, body(): call(first_kernel, (out(81, 8, 128), out(NC, 8, 128), far(BRICKS, 8, 128)...  4.98 us
    ppermute x6, waiting for transfers between devices, swap_pairs(): lax.ppermute(shards[0], axes, inner)  4.56 us
    pallas_call x1, Pallas kernels, body(): call(sweep_kernel, out(NC, 8, 8, 128), [wide_field] * 3 + [pltpu.VMEM((8,...  3.83 us
    pallas_call x1, Pallas kernels, body(): call(rows_kernel, (far(NC, 8, 128), far(BRICKS * SLOT, 128), out(8, 128))...  3.77 us
    ppermute x6, starting transfers between devices, swap_pairs(): lax.ppermute(shards[0], axes, inner)  3.75 us
  transfers between devices with their start and end apart: 14, of which 4 were waited for; matrix products, arithmetic and copies ran while one was open for 0% of the time, Pallas kernels for 24%

profile of v3, /device:TPU:0, one launch (start us, length us, event | category | flops | bytes accessed | tf_op | source)
XLA Modules:
  0.0 58.6 jit_solution(17735207374048810941)
XLA Ops:
  0.6 5.0 %first.1 = (f32[81,8,128]{2,1,0:T(8,128)S(1)}, f32[9,8,128]{2,1,0:T(8,128)S(1)}, f32[16,8,128]{2,1,0:T(8,128)}, f32[576,128]{1,0:T(8,128)S(1)}, f32[1024,128]{1,...) custom-call(s32[8]{0:T(128)} %len_hbm.1, f32[9,8,128]{2,1,0:T(8,128)} %src_hbm.1, ...), custom_call_target="tpu_custom_call" | custom-call | flops 10000000 | bytes 1000000 | tf_op jit(solution)/shard_map/first/pallas_call | solution.py:907
  5.6 7.1 %all-to-all-start = ((f32[16,8,128]{2,1,0:T(8,128)}), f32[16,8,128]{2,1,0:T(8,128)S(1)}, u32[]{:S(2)}, u32[]{:S(2)}) async-start(f32[16,8,128]{2,1,0:T(8,128)} %get-tuple-element.33), calls=%async_computation | async-start | bytes 131072 | tf_op jit(solution)/shard_map/all_to_all | solution.py:938
  12.8 1.9 %collective-permute-start = (f32[1024,128]{1,0:T(8,128)}, f32[1024,128]{1,0:T(8,128)S(1)}, u32[]{:S(2)}, u32[]{:S(2)}) collective-permute-start(f32[1024,128]{1,0:T(8,128)} %get-tuple-element.37), channel_id=1, source_target_pairs={{0,1},{1,0},{2,3},{3,2},{4,5},{5,4},{6,7},{7,6},{8,9},{9,8},{10,11... | collective-permute-start | bytes 1572872 | tf_op jit(solution)/shard_map/ppermute | solution.py:875
  14.7 0.0 collective-permute-start.1
  14.7 0.5 collective-permute-start.2
  15.2 3.6 %collective-permute-start.3 = (f32[936,128]{1,0:T(8,128)}, f32[936,128]{1,0:T(8,128)S(1)}, u32[]{:S(2)}, u32[]{:S(2)}) collective-permute-start(f32[936,128]{1,0:T(8,128)} %get-tuple-element.40), channel_id=1, source_target_pairs={{0,112},{1,113},{2,114},{3,115},{4,116},{5,117},{6,118},{7,119},{8... | collective-permute-start | bytes 1437704 | tf_op jit(solution)/shard_map/ppermute | solution.py:875
  18.8 1.8 %all-to-all-done.heads = f32[16,8,128]{2,1,0:T(8,128)S(1)} async-done(((f32[16,8,128]{2,1,0:T(8,128)}), f32[16,8,128]{2,1,0:T(8,128)S(1)}, u32[]{:S(2)}, u32[]{:S(2)}) %all-to-all-start) | async-done | bytes 65568 | tf_op jit(solution)/shard_map/all_to_all | solution.py:938
  20.7 3.8 %well_rows.1 = (f32[9,8,128]{2,1,0:T(8,128)}, f32[384,128]{1,0:T(8,128)}, f32[8,128]{1,0:T(8,128)S(1)}) custom-call(s32[16]{0:T(128)} %bitcast.17, s32[16,256]{1,0:T(8,128)} %bitcast.16, f32[9,9,16,256]{3,2,1,0:T(8,128)} %bitcast.15, f32[81,8,128]{2,1,0:T(8,128)S(1)} %get-tuple-element.31.mats, f32[9,8,128]{2,1,0:T(8,128)S(1)} %get-tuple-element.32.vecs, ...), custom_call_target="tpu_custom_call" | custom-call | flops 20000000000 | bytes 1000000 | tf_op jit(solution)/shard_map/well_rows/pallas_call | solution.py:942
  24.5 5.8 %all-to-all-start.1 = ((f32[16,24,128]{2,1,0:T(8,128)}), f32[16,24,128]{2,1,0:T(8,128)S(1)}, u32[]{:S(2)}, u32[]{:S(2)}) async-start(f32[16,24,128]{2,1,0:T(8,128)} %bitcast.13), calls=%async_computation.1 | async-start | bytes 393216 | tf_op jit(solution)/shard_map/all_to_all | solution.py:971
  30.3 0.0 collective-permute-done.2.side_a
  30.3 0.0 collective-permute-done.recv_a
  30.3 0.0 collective-permute-done.1.recv_b
  30.3 3.5 %shade.1 = (f32[8,21,24,128]{3,2,1,0:T(8,128)}, f32[1512,128]{1,0:T(8,128)}, f32[1512,128]{1,0:T(8,128)}, f32[576,128]{1,0:T(8,128)}, f32[576,128]{1,0:T(8,128)}) custom-call(f32[8,128]{1,0:T(8,128)S(1)} %get-tuple-element.35.after, f32[9,8,8,128]{3,2,1,0:T(8,128)} %start_hbm.3, f32[8,8,128]{2,1,0:T(8,128)} %px_hbm.3, f32[8,8,128]{2,1,0:T(8,128)} %py_hbm.3, ...), custom_call_target="tpu_custom_call" | custom-call | flops 1000000 | bytes 1000000 | tf_op jit(solution)/shard_map/shade/pallas_call | solution.py:974
  33.9 0.1 collective-permute-start.4
  33.9 1.9 %collective-permute-start.5 = (f32[1512,128]{1,0:T(8,128)}, f32[1512,128]{1,0:T(8,128)S(1)}, u32[]{:S(2)}, u32[]{:S(2)}) collective-permute-start(f32[1512,128]{1,0:T(8,128)} %get-tuple-element.43), channel_id=1, source_target_pairs={{0,112},{1,113},{2,114},{3,115},{4,116},{5,117},{6,118},{7,119},{8... | collective-permute-start | bytes 2322440 | tf_op jit(solution)/shard_map/ppermute | solution.py:875
  35.8 2.8 %all-to-all-done.1.arrived = f32[16,24,128]{2,1,0:T(8,128)S(1)} async-done(((f32[16,24,128]{2,1,0:T(8,128)}), f32[16,24,128]{2,1,0:T(8,128)S(1)}, u32[]{:S(2)}, u32[]{:S(2)}) %all-to-all-start.1) | async-done | bytes 196640 | tf_op jit(solution)/shard_map/all_to_all | solution.py:971
  38.6 3.0 %scatter.1 = (f32[576,128]{1,0:T(8,128)S(1)}, f32[376,128]{1,0:T(8,128)S(1)}, f32[376,128]{1,0:T(8,128)S(1)}, f32[5,9,8,128]{3,2,1,0:T(8,128)S(1)}, f32[5,9,8,128]{3,2,1,0:T(8,128)S(1)}) custom-call(s32[16,2,128]{2,1,0:T(2,128)S(1)} %reshape.35.cell, f32[16,24,128]{2,1,0:T(8,128)S(1)} %all-to-all-done.1.arrived, f32[576,128]{1,0:T(8,128)} %get-tuple-element.49.scale_hbm, ...), custom_call_target="tpu_custom_call" | custom-call | flops 20000000000 | bytes 1000000 | tf_op jit(solution)/shard_map/scatter/pallas_call | solution.py:1001
  41.6 0.6 %collective-permute-start.6 = (f32[376,128]{1,0:T(8,128)S(1)}, f32[376,128]{1,0:T(8,128)S(1)}, u32[]{:S(2)}, u32[]{:S(2)}) collective-permute-start(f32[376,128]{1,0:T(8,128)S(1)} %get-tuple-element.52), channel_id=1, source_target_pairs={{0,1},{1,0},{2,3},{3,2},{4,5},{5,4},{6,7},{7,6},{8,9},{9,8},{10,11... | collective-permute-start | bytes 577544 | tf_op jit(solution)/shard_map/ppermute | solution.py:875
  42.2 0.0 collective-permute-start.7
  42.2 0.5 collective-permute-start.8
  42.7 4.6 %collective-permute-done.6.recv_a = f32[376,128]{1,0:T(8,128)S(1)} collective-permute-done((f32[376,128]{1,0:T(8,128)S(1)}, f32[376,128]{1,0:T(8,128)S(1)}, u32[]{:S(2)}, u32[]{:S(2)}) %collective-permute-start.6) | collective-permute-done | bytes 192544 | tf_op jit(solution)/shard_map/ppermute | solution.py:875
  47.3 0.0 collective-permute-start.9
  47.3 0.0 collective-permute-done.7.recv_b
  47.3 0.1 late_wide.1
  47.4 0.1 collective-permute-start.10
  47.5 0.0 collective-permute-done.4.corner_a
  47.5 3.2 %collective-permute-start.11 = (f32[3,9,8,128]{3,2,1,0:T(8,128)S(1)}, f32[3,9,8,128]{3,2,1,0:T(8,128)S(1)}, u32[]{:S(2)}, u32[]{:S(2)}) collective-permute-start(f32[3,9,8,128]{3,2,1,0:T(8,128)S(1)} %get-tuple-element.59), channel_id=1, source_target_pairs={{0,112},{1,113},{2,114},{3,115},{4,116},{5,117},{6,118},{7,119},{8... | collective-permute-start | bytes 331784 | tf_op jit(solution)/shard_map/ppermute | solution.py:875
  50.7 3.6 %early.1 = (f32[18,6,16,128]{3,2,1,0:T(8,128)S(1)}, f32[18,9,16,128]{3,2,1,0:T(8,128)S(1)}, f32[18,9,16,128]{3,2,1,0:T(8,128)S(1)}, f32[8,9,8,128]{3,2,1,0:T(8,128)S(1)}) custom-call(f32[8,21,24,128]{3,2,1,0:T(8,128)} %get-tuple-element.41.wide_hbm, f32[936,128]{1,0:T(8,128)S(1)} %collective-permute-done.2.side_a, ...), custom_call_target="tpu_custom_call" | custom-call | flops 1000000 | bytes 1000000 | tf_op jit(solution)/shard_map/early/pallas_call | solution.py:1027
  54.3 0.0 collective-permute-done.8.side_a
  54.3 0.0 collective-permute-done.10.corner_a
  54.3 0.3 collective-permute-done.11.corner_b
  54.6 3.8 %sweeps.1 = f32[9,8,8,128]{3,2,1,0:T(8,128)} custom-call(f32[18,6,16,128]{3,2,1,0:T(8,128)S(1)} %get-tuple-element.44.trans, f32[18,9,16,128]{3,2,1,0:T(8,128)S(1)} %get-tuple-element.45.gain, f32[18,9,16,128]{3,2,1,0:T(8,128)S(1)} %get-tuple-element.46.begin, f32[8,9,8,128]{3,2,1,0:T(8,128)S(1)} %get-tuple-element.47.begin_edge, ...), custom_call_target="tpu_custom_call" | custom-call | flops 1000000 | bytes 1000000 | tf_op jit(solution)/shard_map/sweeps/pallas_call | solution.py:1062
  (6 shorter events, 0.0 us)
Async XLA Ops:
  5.6 15.1 %all-to-all-start = ((f32[16,8,128]{2,1,0:T(8,128)}), f32[16,8,128]{2,1,0:T(8,128)S(1)}, u32[]{:S(2)}, u32[]{:S(2)}) async-start(f32[16,8,128]{2,1,0:T(8,128)} %get-tuple-element.33), calls=%async_computation | async-start | bytes 131072 | tf_op jit(solution)/shard_map/all_to_all | solution.py:938
  12.8 17.6 %collective-permute-start = (f32[1024,128]{1,0:T(8,128)}, f32[1024,128]{1,0:T(8,128)S(1)}, u32[]{:S(2)}, u32[]{:S(2)}) collective-permute-start(f32[1024,128]{1,0:T(8,128)} %get-tuple-element.37), channel_id=1, source_target_pairs={{0,1},{1,0},{2,3},{3,2},{4,5},{5,4},{6,7},{7,6},{8,9},{9,8},{10,11... | collective-permute-start | bytes 1572872 | tf_op jit(solution)/shard_map/ppermute | solution.py:875
  14.7 15.7 %collective-permute-start.1 = (f32[1024,128]{1,0:T(8,128)}, f32[1024,128]{1,0:T(8,128)S(1)}, u32[]{:S(2)}, u32[]{:S(2)}) collective-permute-start(f32[1024,128]{1,0:T(8,128)} %get-tuple-element.38), channel_id=1, source_target_pairs={{0,16},{1,2},{2,1},{3,4},{4,3},{5,6},{6,5},{7,8},{8,7},{9,10},{10,... | collective-permute-start | bytes 1572872 | tf_op jit(solution)/shard_map/ppermute | solution.py:875
  14.7 15.6 %collective-permute-start.2 = (f32[936,128]{1,0:T(8,128)}, f32[936,128]{1,0:T(8,128)S(1)}, u32[]{:S(2)}, u32[]{:S(2)}) collective-permute-start(f32[936,128]{1,0:T(8,128)} %get-tuple-element.39), channel_id=1, source_target_pairs={{0,16},{1,17},{2,18},{3,19},{4,20},{5,21},{6,22},{7,23},{8,24},{9,... | collective-permute-start | bytes 1437704 | tf_op jit(solution)/shard_map/ppermute | solution.py:875
  15.2 15.1 %collective-permute-start.3 = (f32[936,128]{1,0:T(8,128)}, f32[936,128]{1,0:T(8,128)S(1)}, u32[]{:S(2)}, u32[]{:S(2)}) collective-permute-start(f32[936,128]{1,0:T(8,128)} %get-tuple-element.40), channel_id=1, source_target_pairs={{0,112},{1,113},{2,114},{3,115},{4,116},{5,117},{6,118},{7,119},{8... | collective-permute-start | bytes 1437704 | tf_op jit(solution)/shard_map/ppermute | solution.py:875
  20.7 9.6 %copy-start = (s32[1,1,16,256]{3,2,1,0:T(8,128)S(1)}, s32[1,1,16,256]{3,2,1,0:T(8,128)}, u32[]{:S(2)}) copy-start(s32[1,1,16,256]{3,2,1,0:T(8,128)} %param.22) | copy-start | bytes 49156
  24.5 14.2 %all-to-all-start.1 = ((f32[16,24,128]{2,1,0:T(8,128)}), f32[16,24,128]{2,1,0:T(8,128)S(1)}, u32[]{:S(2)}, u32[]{:S(2)}) async-start(f32[16,24,128]{2,1,0:T(8,128)} %bitcast.13), calls=%async_computation.1 | async-start | bytes 393216 | tf_op jit(solution)/shard_map/all_to_all | solution.py:971
  33.9 13.7 %collective-permute-start.4 = (f32[1512,128]{1,0:T(8,128)}, f32[1512,128]{1,0:T(8,128)S(1)}, u32[]{:S(2)}, u32[]{:S(2)}) collective-permute-start(f32[1512,128]{1,0:T(8,128)} %get-tuple-element.42), channel_id=1, source_target_pairs={{0,16},{1,17},{2,18},{3,19},{4,20},{5,21},{6,22},{7,23},{8,24},{9,... | collective-permute-start | bytes 2322440 | tf_op jit(solution)/shard_map/ppermute | solution.py:875
  33.9 16.8 %collective-permute-start.5 = (f32[1512,128]{1,0:T(8,128)}, f32[1512,128]{1,0:T(8,128)S(1)}, u32[]{:S(2)}, u32[]{:S(2)}) collective-permute-start(f32[1512,128]{1,0:T(8,128)} %get-tuple-element.43), channel_id=1, source_target_pairs={{0,112},{1,113},{2,114},{3,115},{4,116},{5,117},{6,118},{7,119},{8... | collective-permute-start | bytes 2322440 | tf_op jit(solution)/shard_map/ppermute | solution.py:875
  41.6 5.7 %collective-permute-start.6 = (f32[376,128]{1,0:T(8,128)S(1)}, f32[376,128]{1,0:T(8,128)S(1)}, u32[]{:S(2)}, u32[]{:S(2)}) collective-permute-start(f32[376,128]{1,0:T(8,128)S(1)} %get-tuple-element.52), channel_id=1, source_target_pairs={{0,1},{1,0},{2,3},{3,2},{4,5},{5,4},{6,7},{7,6},{8,9},{9,8},{10,11... | collective-permute-start | bytes 577544 | tf_op jit(solution)/shard_map/ppermute | solution.py:875
  42.2 5.1 %collective-permute-start.7 = (f32[376,128]{1,0:T(8,128)S(1)}, f32[376,128]{1,0:T(8,128)S(1)}, u32[]{:S(2)}, u32[]{:S(2)}) collective-permute-start(f32[376,128]{1,0:T(8,128)S(1)} %get-tuple-element.53), channel_id=1, source_target_pairs={{0,16},{1,2},{2,1},{3,4},{4,3},{5,6},{6,5},{7,8},{8,7},{9,10},{10,... | collective-permute-start | bytes 577544 | tf_op jit(solution)/shard_map/ppermute | solution.py:875
  42.2 12.1 %collective-permute-start.8 = (f32[5,9,8,128]{3,2,1,0:T(8,128)S(1)}, f32[5,9,8,128]{3,2,1,0:T(8,128)S(1)}, u32[]{:S(2)}, u32[]{:S(2)}) collective-permute-start(f32[5,9,8,128]{3,2,1,0:T(8,128)S(1)} %get-tuple-element.56), channel_id=1, source_target_pairs={{0,16},{1,17},{2,18},{3,19},{4,20},{5,21},{6,22},{7,23},{8,24},{9,... | collective-permute-start | bytes 552968 | tf_op jit(solution)/shard_map/ppermute | solution.py:875
  47.3 7.0 %collective-permute-start.9 = (f32[5,9,8,128]{3,2,1,0:T(8,128)S(1)}, f32[5,9,8,128]{3,2,1,0:T(8,128)S(1)}, u32[]{:S(2)}, u32[]{:S(2)}) collective-permute-start(f32[5,9,8,128]{3,2,1,0:T(8,128)S(1)} %get-tuple-element.57), channel_id=1, source_target_pairs={{0,112},{1,113},{2,114},{3,115},{4,116},{5,117},{6,118},{7,119},{8... | collective-permute-start | bytes 552968 | tf_op jit(solution)/shard_map/ppermute | solution.py:875
  47.4 6.9 %collective-permute-start.10 = (f32[3,9,8,128]{3,2,1,0:T(8,128)S(1)}, f32[3,9,8,128]{3,2,1,0:T(8,128)S(1)}, u32[]{:S(2)}, u32[]{:S(2)}) collective-permute-start(f32[3,9,8,128]{3,2,1,0:T(8,128)S(1)} %get-tuple-element.58), channel_id=1, source_target_pairs={{0,16},{1,17},{2,18},{3,19},{4,20},{5,21},{6,22},{7,23},{8,24},{9,... | collective-permute-start | bytes 331784 | tf_op jit(solution)/shard_map/ppermute | solution.py:875
  47.5 7.1 %collective-permute-start.11 = (f32[3,9,8,128]{3,2,1,0:T(8,128)S(1)}, f32[3,9,8,128]{3,2,1,0:T(8,128)S(1)}, u32[]{:S(2)}, u32[]{:S(2)}) collective-permute-start(f32[3,9,8,128]{3,2,1,0:T(8,128)S(1)} %get-tuple-element.59), channel_id=1, source_target_pairs={{0,112},{1,113},{2,114},{3,115},{4,116},{5,117},{6,118},{7,119},{8... | collective-permute-start | bytes 331784 | tf_op jit(solution)/shard_map/ppermute | solution.py:875
